TPU v7x, 256 devices: a whole 4x4x8 slice. The times are simulated.
256 devices in a mesh: gx: 16 (over z, core), gy: 16 (over x, y).
Axes of the slice: x: 4, y: 4, z: 8, core: 2. Of those that a mesh axis runs over, the one named last changes fastest.
Arguments:
- velocity: float32 [3, 2, 5, 5, 5, 16, 16, 256], P(None, None, None, None, None, 'gx', 'gy'), may hold values from -6 to 6
- convecting: float32 [3, 2, 5, 5, 5, 16, 16, 256], P(None, None, None, None, None, 'gx', 'gy'), may hold values from -6 to 6
- donor_element: int32 [25600], P(('gx', 'gy')), may hold values from 0 to 511
- coords: float32 [3, 25600], P(None, ('gx', 'gy')), may hold values from -1 to 1
- dest_rank: int32 [25600], P(('gx', 'gy')), may hold values from 0 to 255, as said below
- target: int32 [25600], P(('gx', 'gy')), may hold values from 0 to 99, as said below
Outputs:
- advected: float32 [3, 2, 5, 5, 5, 16, 16, 256], P(None, None, None, None, None, 'gx', 'gy')
Inputs may be any that keep to these rules, and one draw needn't show every extreme that they name: Every interface point of every device is named by exactly one query, through dest_rank and target together. `dest_rank`: the queries held by one device name each device at most 1 times, and some device exactly that often.
All inputs are finite; a program needn't handle non-finite values.
Results may differ from a plain program's by a relative error of at most 0.0001.
Values sent between devices are 32-bit elements; how exact they have to be, the bound alone decides.
No kernel may reach another device: no remote copies, remote signals or barrier semaphores. Data moves between devices by JAX's collectives and lax.ppermute only.
A program may use at most 64 MiB of HBM per device.

v0:
```python
import functools
import math

import jax
import jax.numpy as jnp
import numpy as np
from jax import lax
from jax.experimental import pallas as pl
from jax.experimental.pallas import tpu as pltpu
from jax.sharding import PartitionSpec as P

time_step = 0.04
NP = 5
PTS = NP * NP * NP
ROWS = 6
EZ = 256
SLOT = 8
f32 = jnp.float32


def gll_tables():
    root_value = math.sqrt(3.0 / 7.0)
    nodes = [-1.0, -root_value, 0.0, root_value, 1.0]
    bary = []
    for i in range(NP):
        product = 1.0
        for j in range(NP):
            if j != i:
                product = product * (nodes[i] - nodes[j])
        bary.append(1.0 / product)
    table = np.zeros((NP, NP))
    for a in range(NP):
        for i in range(NP):
            if a != i:
                table[a, i] = bary[i] / bary[a] / (nodes[a] - nodes[i])
        table[a, a] = -np.sum(table[a])
    return nodes, table


NODES, D = gll_tables()


def pt(i, j, k):
    return (i * NP + j) * NP + k


def line_derivative(u):
    d0, d1 = u[0] - u[4], u[1] - u[3]
    s0, s1 = u[0] + u[4], u[1] + u[3]
    out = [None] * NP
    out[2] = d0 * float(D[2, 0]) + d1 * float(D[2, 1])
    for a in (0, 1):
        odd = d0 * float((D[a, 0] - D[a, 4]) / 2) + d1 * float((D[a, 1] - D[a, 3]) / 2)
        even = (
            s0 * float((D[a, 0] + D[a, 4]) / 2)
            + s1 * float((D[a, 1] + D[a, 3]) / 2)
            + u[2] * float(D[a, 2])
        )
        out[a] = odd + even
        out[4 - a] = odd - even
    return out


def end_derivatives(u):
    d0, d1 = u[0] - u[4], u[1] - u[3]
    s0, s1 = u[0] + u[4], u[1] + u[3]
    odd = d0 * float((D[0, 0] - D[0, 4]) / 2) + d1 * float((D[0, 1] - D[0, 3]) / 2)
    even = (
        s0 * float((D[0, 0] + D[0, 4]) / 2)
        + s1 * float((D[0, 1] + D[0, 3]) / 2)
        + u[2] * float(D[0, 2])
    )
    return odd + even, odd - even


def lane_index():
    return lax.broadcasted_iota(jnp.int32, (ROWS, EZ), 1)


def row_index():
    return lax.broadcasted_iota(jnp.int32, (ROWS, EZ), 0)


def place():
    a, b = lax.axis_index("gx"), lax.axis_index("gy")
    n, m = lax.axis_size("gx"), lax.axis_size("gy")
    ea, eb = a % 2 == 0, b % 2 == 0
    ia, ja = jnp.where(ea, 4, 0), jnp.where(eb, 4, 0)
    sx = jnp.where((a == 0) | (a == n - 1), 0.0, 1.0).astype(f32)
    sy = jnp.where((b == 0) | (b == m - 1), 0.0, 1.0).astype(f32)
    return a, b, n, m, ea, eb, ia, ja, sx, sy


def widen(two, odd_row):
    return jnp.where(odd_row, two[1:2], two[0:1])


def z_sum(ref, ij):
    low, high = ref[ij * NP], ref[ij * NP + 4]
    ref[ij * NP] = low + pltpu.roll(high, 1, 1)
    ref[ij * NP + 4] = high + pltpu.roll(low, EZ - 1, 1)


def first_kernel(vel, conv, u8, c0, c1, c2, w, xa, xb):
    a, b, n, m, ea, eb, ia, ja, sx, sy = place()
    lane, odd_row = lane_index(), row_index() % 2 == 1
    hx = {0: jnp.where(a > 0, 0.5, 1.0), 4: jnp.where(a < n - 1, 0.5, 1.0)}
    hy = {0: jnp.where(b > 0, 0.5, 1.0), 4: jnp.where(b < m - 1, 0.5, 1.0)}
    one = jnp.full((ROWS, EZ), -1.0, f32)
    hz = {
        0: jnp.where(lane == 0, 0.0, -0.5).astype(f32),
        4: jnp.where(lane == EZ - 1, 0.0, -0.5).astype(f32),
    }
    for i in range(NP):
        for j in range(NP):
            side = hx.get(i, 1.0) * hy.get(j, 1.0)
            for k in range(NP):
                p = pt(i, j, k)
                scale = hz.get(k, one)
                if i in hx or j in hy:
                    scale = scale * side.astype(f32)
                cc = conv[p] * scale
                c0[p] = widen(cc[0:2], odd_row)
                c1[p] = widen(cc[2:4], odd_row)
                c2[p] = widen(cc[4:6], odd_row)
                u8[p, 0:ROWS] = vel[p]
    for j in range(NP):
        for k in range(NP):
            g = line_derivative([vel[pt(i, j, k)] for i in range(NP)])
            for i in range(NP):
                w[pt(i, j, k)] = c0[pt(i, j, k)] * g[i]
    for i in range(NP):
        for k in range(NP):
            g = line_derivative([vel[pt(i, j, k)] for j in range(NP)])
            for j in range(NP):
                w[pt(i, j, k)] += c1[pt(i, j, k)] * g[j]
    for i in range(NP):
        for j in range(NP):
            u = [vel[pt(i, j, k)] for k in range(NP)]
            u[0] = jnp.where(lane == 0, 0.0, u[0])
            u[4] = jnp.where(lane == EZ - 1, 0.0, u[4])
            g = line_derivative(u)
            for k in range(NP):
                w[pt(i, j, k)] += c2[pt(i, j, k)] * g[k]
    for jk in range(NP * NP):
        pa, pb = ia * 25 + jk, (4 - ia) * 25 + jk
        xa[jk * 10 : jk * 10 + 6] = w[pa]
        xa[jk * 10 + 6 : jk * 10 + 8] = c1[pa, 0:2]
        xa[jk * 10 + 8 : jk * 10 + 10] = c2[pa, 0:2]
        xb[jk * 10 : jk * 10 + 6] = w[pb] * sx
        xb[jk * 10 + 6 : jk * 10 + 8] = c1[pb, 0:2] * sx
        xb[jk * 10 + 8 : jk * 10 + 10] = c2[pb, 0:2] * sx


def second_kernel(w, c0, c2, xa, xb, ya, yb):
    a, b, n, m, ea, eb, ia, ja, sx, sy = place()

    def edge(j_even, k, lo, hi, low_side):
        def at(j):
            r = (j * NP + k) * 10
            from_a, from_b = xa[r + lo : r + hi], xb[r + lo : r + hi]
            return jnp.where(ea, from_b, from_a) if low_side else jnp.where(ea, from_a, from_b)

        return jnp.where(j_even, at(4), at(0))

    for dst, jf, j_even, scale in ((ya, ja, eb, None), (yb, 4 - ja, jnp.logical_not(eb), sy)):
        put = (lambda x: x) if scale is None else (lambda x: x * scale)
        for i in range(NP):
            for k in range(NP):
                p = i * 25 + jf * NP + k
                r = (i * NP + k) * 10
                face = w[p]
                if i in (0, 4):
                    face = face + edge(j_even, k, 0, 6, i == 0)
                dst[r : r + 6] = put(face)
                dst[r + 6 : r + 8] = put(c0[p, 0:2])
                dst[r + 8 : r + 10] = put(c2[p, 0:2])
        for k in range(NP):
            for s, low_side in ((0, True), (1, False)):
                r = 250 + (s * NP + k) * 2
                dst[r : r + 2] = put(edge(j_even, k, 8, 10, low_side))


def query_kernel(u8, donor, coords, dest, target, table):
    queries = donor.shape[1]
    devices = table.shape[0]
    n, m = lax.axis_size("gx"), lax.axis_size("gy")
    lane_elem = donor[...] & (EZ - 1)
    hot = (
        lax.broadcasted_iota(jnp.int32, (EZ, queries), 0) == jnp.broadcast_to(lane_elem, (EZ, queries))
    ).astype(f32)
    grid = jnp.dot(
        u8[...].reshape(PTS * 8, EZ),
        hot,
        precision=lax.Precision.HIGHEST,
        preferred_element_type=f32,
    ).reshape(PTS, 8, queries)
    basis = []
    for d in range(3):
        x = coords[d : d + 1]
        line = []
        for i in range(NP):
            v = jnp.ones_like(x)
            for j in range(NP):
                if j != i:
                    v = v * ((x - NODES[j]) * (1.0 / (NODES[i] - NODES[j])))
            line.append(v)
        basis.append(line)
    total = jnp.zeros((8, queries), f32)
    for i in range(NP):
        for j in range(NP):
            part = grid[pt(i, j, 0)] * basis[2][0]
            for k in range(1, NP):
                part = part + grid[pt(i, j, k)] * basis[2][k]
            total = total + part * (basis[0][i] * basis[1][j])
    low = donor[...] < EZ
    rows = [jnp.where(low, total[2 * c : 2 * c + 1], total[2 * c + 1 : 2 * c + 2]) for c in range(3)]
    rows.append((target[...] + 1).astype(f32))
    row = lax.broadcasted_iota(jnp.int32, (8, queries), 0)
    packed = jnp.zeros((8, queries), f32)
    for r, x in enumerate(rows):
        packed = jnp.where(row == r, jnp.broadcast_to(x, (8, queries)), packed)
    goes = (
        lax.broadcasted_iota(jnp.int32, (devices, queries), 0)
        == jnp.broadcast_to(dest[...], (devices, queries))
    ).astype(f32)
    mine = lax.dot_general(
        packed,
        goes,
        (((1,), (1,)), ((), ())),
        precision=lax.Precision.HIGHEST,
        preferred_element_type=f32,
    )
    device = lax.broadcasted_iota(jnp.int32, (8, devices), 1)
    da, db = device // m, device % m

    def partner(x, pos, last, stride, first):
        even = pos % 2 == 0
        ahead, behind = pltpu.roll(x, devices - stride, 1), pltpu.roll(x, stride, 1)
        if first:
            return jnp.where(even, ahead, behind)
        return jnp.where((pos == 0) | (pos == last), 0.0, jnp.where(even, behind, ahead))

    x_a, x_b = partner(mine, da, n - 1, m, True), partner(mine, da, n - 1, m, False)
    slots = [mine, x_a, x_b]
    for first in (True, False):
        slots += [partner(s, db, m - 1, 1, first) for s in (mine, x_a, x_b)]
    slots.append(jnp.zeros((128 - SLOT * 9, devices), f32))
    table[...] = jnp.concatenate(slots, axis=0).T


def third_kernel(w_in, c0_in, c1_in, c2_in, u8, xa, xb, ya, yb, table, v, c0, c1, c2, acc, oxa, oxb, oya, oyb, z):
    a, b, n, m, ea, eb, ia, ja, sx, sy = place()
    del w_in, c0_in, c1_in, c2_in
    lane, row = lane_index(), row_index()
    odd_row = row % 2 == 1
    got = table[...].T
    base = (row % 2) * 50 + 1
    slope = [
        jnp.where(lane < EZ // 2, float(D[k, 0]), float(D[k, 4])).astype(f32) for k in range(NP)
    ]

    def values(slot, points):
        r = slot * SLOT
        mine = jnp.where(row < 2, got[r : r + 1], jnp.where(row < 4, got[r + 1 : r + 2], got[r + 2 : r + 3]))
        key = got[r + 3 : r + 4] - base.astype(f32)
        for where, ij in points:
            ends = []
            for side in range(2):
                hit = key == jnp.asarray(side * 25 + ij).astype(f32)
                ends.append(jnp.sum(jnp.where(hit, mine, 0.0), axis=1, keepdims=True))
            z[where] = jnp.where(lane == 0, ends[0], jnp.where(lane == EZ - 1, ends[1], 0.0))

    ib, jb = 4 - ia, 4 - ja
    values(0, [(ij, ij) for ij in range(25)])
    values(1, [(25 + j, ib * NP + j) for j in range(NP)])
    values(2, [(30 + j, ia * NP + j) for j in range(NP)])
    values(3, [(35 + i, i * NP + jb) for i in range(NP)])
    values(6, [(40 + i, i * NP + ja) for i in range(NP)])
    values(4, [(45, ib * NP + jb)])
    values(5, [(46, ia * NP + jb)])
    values(7, [(47, ib * NP + ja)])
    values(8, [(48, ia * NP + ja)])

    for ij in range(25):
        zz = z[ij]
        for k in range(NP):
            p = ij * NP + k
            v[p] += c2[p] * (zz * slope[k])
            u = u8[p, 0:ROWS]
            if k == 0:
                u = jnp.where(lane == 0, zz, u)
            if k == 4:
                u = jnp.where(lane == EZ - 1, zz, u)
            acc[p] = u
    for src, face, z0 in ((xa, ia, 25), (xb, ib, 30)):
        for j in range(NP):
            zz = z[z0 + j]
            for k in range(NP):
                r = (j * NP + k) * 10
                p = face * 25 + j * NP + k
                extra = widen(src[r + 8 : r + 10], odd_row)
                v[p] += src[r : r + 6] + extra * (zz * slope[k])
                c1[p] += widen(src[r + 6 : r + 8], odd_row)
                c2[p] += extra
    for src, face, z0, zd in ((ya, ja, 35, 45), (yb, jb, 40, 47)):
        for i in range(NP):
            zz = z[z0 + i]
            for k in range(NP):
                r = (i * NP + k) * 10
                p = i * 25 + face * NP + k
                extra = widen(src[r + 8 : r + 10], odd_row)
                add = src[r : r + 6] + extra * (zz * slope[k])
                if i in (0, 4):
                    r = 250 + ((i // 4) * NP + k) * 2
                    far = widen(src[r : r + 2], odd_row)
                    through_a = ea if i == 4 else jnp.logical_not(ea)
                    zfar = jnp.where(through_a, z[zd], z[zd + 1])
                    add = add + far * (zfar * slope[k])
                    extra = extra + far
                v[p] += add
                c0[p] += widen(src[(i * NP + k) * 10 + 6 : (i * NP + k) * 10 + 8], odd_row)
                c2[p] += extra
    for ij in range(25):
        z_sum(v, ij)
        z_sum(c0, ij)
        z_sum(c1, ij)
    messages(v, c0, c1, oxa, oxb, oya, oyb)


def messages(v, c0, c1, oxa, oxb, oya, oyb):
    a, b, n, m, ea, eb, ia, ja, sx, sy = place()
    for i in range(NP):
        for k in range(NP):
            low, high = end_derivatives([v[pt(i, j, k)] for j in range(NP)])
            low, high = low * c1[pt(i, 0, k)], high * c1[pt(i, 4, k)]
            r = (i * NP + k) * 6
            oya[r : r + 6] = jnp.where(eb, high, low)
            oyb[r : r + 6] = jnp.where(eb, low, high) * sy
    for j in range(NP):
        for k in range(NP):
            low, high = end_derivatives([v[pt(i, j, k)] for i in range(NP)])
            low, high = low * c0[pt(0, j, k)], high * c0[pt(4, j, k)]
            r = (j * NP + k) * 6
            oxa[r : r + 6] = jnp.where(ea, high, low)
            oxb[r : r + 6] = jnp.where(ea, low, high) * sx


def take_messages(v, xa, xb, ya, yb):
    a, b, n, m, ea, eb, ia, ja, sx, sy = place()
    for src, face in ((xa, ia), (xb, 4 - ia)):
        for jk in range(25):
            v[face * 25 + jk] += src[jk * 6 : jk * 6 + 6]
    for src, face in ((ya, ja), (yb, 4 - ja)):
        for i in range(NP):
            for k in range(NP):
                r = (i * NP + k) * 6
                v[i * 25 + face * NP + k] += src[r : r + 6]


def send_kernel(w_in, c0, c1, xa, xb, ya, yb, v, oxa, oxb, oya, oyb):
    del w_in
    take_messages(v, xa, xb, ya, yb)
    messages(v, c0, c1, oxa, oxb, oya, oyb)


def local_kernel(coef, v, c0, c1, c2, acc_in, acc, w):
    del acc_in
    for j in range(NP):
        for k in range(NP):
            u = [v[pt(i, j, k)] for i in range(NP)]
            g = line_derivative(u)
            for i in range(NP):
                p = pt(i, j, k)
                acc[p] += u[i] * coef
                w[p] = c0[p] * g[i]
    for i in range(NP):
        for k in range(NP):
            g = line_derivative([v[pt(i, j, k)] for j in range(NP)])
            for j in range(NP):
                w[pt(i, j, k)] += c1[pt(i, j, k)] * g[j]
    for i in range(NP):
        for j in range(NP):
            g = line_derivative([v[pt(i, j, k)] for k in range(NP)])
            t = [c2[pt(i, j, k)] * g[k] for k in range(NP)]
            t[0], t[4] = t[0] + pltpu.roll(t[4], 1, 1), t[4] + pltpu.roll(t[0], EZ - 1, 1)
            for k in range(NP):
                w[pt(i, j, k)] += t[k]


def last_kernel(coef, w_in, acc, xa, xb, ya, yb, v, out):
    del w_in
    take_messages(v, xa, xb, ya, yb)
    for p in range(PTS):
        out[p] = acc[p] + v[p] * coef


FIELD = (PTS, ROWS, EZ)


def call(kernel, outs, args, aliases=None, scratch=(), flops=0):
    moved = sum(4 * math.prod(x.shape) for x in args) + sum(4 * math.prod(s) for s in outs)
    return pl.pallas_call(
        kernel,
        out_shape=[jax.ShapeDtypeStruct(s, f32) for s in outs],
        in_specs=[pl.BlockSpec(memory_space=pltpu.VMEM)] * len(args),
        out_specs=[pl.BlockSpec(memory_space=pltpu.VMEM)] * len(outs),
        input_output_aliases=aliases or {},
        scratch_shapes=list(scratch),
        compiler_params=pltpu.CompilerParams(vmem_limit_bytes=24 * 1024 * 1024),
        cost_estimate=pl.CostEstimate(flops=flops, bytes_accessed=moved, transcendentals=0),
    )(*args)


def pairs(size, offset):
    route = []
    for low in range(offset, size, 2):
        high = (low + 1) % size
        route += [(low, high), (high, low)]
    return route


def swap(x, axis, offset):
    return lax.ppermute(x, axis, pairs(lax.axis_size(axis), offset))


def swap_all(xa, xb, ya, yb):
    return swap(xa, "gx", 0), swap(xb, "gx", 1), swap(ya, "gy", 0), swap(yb, "gy", 1)


def body(velocity, convecting, donor_element, coords, dest_rank, target):
    devices = lax.axis_size("gx") * lax.axis_size("gy")
    queries = dest_rank.shape[0]
    vel = jnp.transpose(velocity.reshape(ROWS, PTS, EZ), (1, 0, 2))
    conv = jnp.transpose(convecting.reshape(ROWS, PTS, EZ), (1, 0, 2))
    u8, c0, c1, c2, w, xa, xb = call(
        first_kernel, [(PTS, 8, EZ)] + [FIELD] * 4 + [(250, EZ)] * 2, [vel, conv]
    )
    xa, xb = swap(xa, "gx", 0), swap(xb, "gx", 1)
    (table,) = call(
        query_kernel,
        [(devices, 128)],
        [
            u8,
            donor_element.reshape(1, queries),
            coords,
            dest_rank.reshape(1, queries),
            target.reshape(1, queries),
        ],
    )
    ya, yb = call(second_kernel, [(270, EZ)] * 2, [w, c0, c2, xa, xb])
    table, ya, yb = lax.optimization_barrier((table, ya, yb))
    ya, yb = swap(ya, "gy", 0), swap(yb, "gy", 1)
    table = lax.all_to_all(table.reshape(devices, 1, 128), ("gx", "gy"), 0, 0).reshape(devices, 128)
    v, c0, c1, c2, acc, oxa, oxb, oya, oyb = call(
        third_kernel,
        [FIELD] * 5 + [(150, EZ)] * 4,
        [w, c0, c1, c2, u8, xa, xb, ya, yb, table],
        aliases={0: 0, 1: 1, 2: 2, 3: 3},
        scratch=[pltpu.VMEM((49, ROWS, EZ), f32)],
    )
    coef = 1.0
    for stage in range(1, 4):
        coef = coef * time_step / stage
        got = swap_all(oxa, oxb, oya, oyb)
        acc, w = call(
            functools.partial(local_kernel, coef),
            [FIELD] * 2,
            [v, c0, c1, c2, acc],
            aliases={4: 0},
            flops=10**7,
        )
        if stage < 3:
            v, oxa, oxb, oya, oyb = call(
                send_kernel, [FIELD] + [(150, EZ)] * 4, [w, c0, c1, *got], aliases={0: 0}
            )
    coef = coef * time_step / 4
    _, out = call(
        functools.partial(last_kernel, coef), [FIELD] * 2, [w, acc, *got], aliases={0: 0}
    )
    return jnp.transpose(out, (1, 0, 2)).reshape(velocity.shape)


def solution(mesh):
    field = P(None, None, None, None, None, "gx", "gy", None)
    return jax.shard_map(
        body,
        mesh=mesh,
        in_specs=(field, field, P(("gx", "gy")), P(None, ("gx", "gy")), P(("gx", "gy")), P(("gx", "gy"))),
        out_specs=field,
        check_vma=False,
    )
```

profile of v0, /device:TPU:1, one launch (start us, length us, event | category | flops | bytes accessed | tf_op | source)
XLA Modules:
  0.0 82.1 jit_solution(4551294516798758400)
XLA Ops:
  0.0 3.0 %reduce = f32[3,2,5,5,5,256]{5,4,3,2,1,0:T(8,128)S(1)} reduce(f32[3,2,5,5,5,1,1,256]{7,6,5,4,3,2,1,0:T(1,128)} %param.6, f32[]{:T(128)} %constant.6), dimensions={5,6}, to_apply=%param.6.reduce_sub_computation | reduce | bytes 1536004 | tf_op args[0]
  3.0 0.0 copy-start.4
  3.0 0.1 reshape.32
  3.1 1.0 %copy-done.4 = f32[3,2,5,5,5,1,1,256]{7,6,5,4,3,2,1,0:T(1,128)S(1)} copy-done((f32[3,2,5,5,5,1,1,256]{7,6,5,4,3,2,1,0:T(1,128)S(1)}, f32[3,2,5,5,5,1,1,256]{7,6,5,4,3,2,1,0:T(1,128)}, u32[]{:S(2)}) %copy-start.4) | copy-done | bytes 768024
  4.1 1.8 %reduce.1 = f32[3,2,5,5,5,256]{5,4,3,2,1,0:T(8,128)S(1)} reduce(f32[3,2,5,5,5,1,1,256]{7,6,5,4,3,2,1,0:T(1,128)S(1)} %copy-done.4, f32[]{:T(128)} %constant.6), dimensions={5,6}, to_apply=%param.7.reduce_sub_computation | reduce | bytes 1536004 | tf_op args[1]
  6.0 0.1 reshape.33
  6.1 0.9 %copy_bitcast_fusion = (f32[125,6,256]{2,1,0:T(8,128)S(1)}, f32[125,6,256]{2,1,0:T(8,128)S(1)}) fusion(f32[6,125,256]{2,1,0:T(8,128)S(1)} %reshape.33, f32[6,125,256]{2,1,0:T(8,128)S(1)} %reshape.32), kind=kLoop, calls=%fused_computation | loop fusion | bytes 3072000 | tf_op jit(solution)/shard_map/transpose | solution.py:435
  7.0 0.0 copy-start
  7.1 0.0 copy-start.1
  7.1 0.0 copy-start.2
  7.1 0.0 copy-start.3
  7.1 1.5 %shard_map.64 = (f32[125,8,256]{2,1,0:T(8,128)S(1)}, f32[125,6,256]{2,1,0:T(8,128)S(1)}, f32[125,6,256]{2,1,0:T(8,128)S(1)}, f32[125,6,256]{2,1,0:T(8,128)S(1)},...) custom-call(f32[125,6,256]{2,1,0:T(8,128)S(1)} %get-tuple-element.82.vel, ...), custom_call_target="tpu_custom_call" | custom-call | bytes 6144000 | tf_op jit(solution)/shard_map/pallas_call | solution.py:403
  8.6 3.3 %collective-permute-start = (f32[250,256]{1,0:T(8,128)S(1)}, f32[250,256]{1,0:T(8,128)S(1)}, u32[]{:S(2)}, u32[]{:S(2)}) collective-permute-start(f32[250,256]{1,0:T(8,128)S(1)} %get-tuple-element.48), channel_id=1, source_target_pairs={{0,16},{16,0},{32,48},{48,32},{64,80},{80,64},{96,112},{112,96},{1... | collective-permute-start | bytes 768008 | tf_op jit(solution)/shard_map/ppermute | solution.py:424
  11.9 0.0 collective-permute-start.1
  11.9 0.0 copy-done
  12.0 0.0 copy-done.1
  12.0 0.0 copy-done.2
  12.0 0.0 copy-done.3
  12.0 1.6 %shard_map.65 = f32[256,128]{1,0:T(8,128)S(1)} custom-call(f32[125,8,256]{2,1,0:T(8,128)S(1)} %get-tuple-element.47.u8, s32[1,100]{1,0:T(1,128)S(1)} %bitcast.17, f32[3,100]{1,0:T(4,128)S(1)} %copy-done, s32[1,100]{1,0:T(1,128)S(1)} %bitcast.18, s32[1,100]{1,0:T(1,128)S(1)} %bitcast.19), custom_call_target="tpu_custom_call" | custom-call | bytes 1157472 | tf_op jit(solution)/shard_map/pallas_call | solution.py:403
  13.6 0.0 collective-permute-done.xa
  13.6 4.5 %collective-permute-done.1.xb = f32[250,256]{1,0:T(8,128)S(1)} collective-permute-done((f32[250,256]{1,0:T(8,128)S(1)}, f32[250,256]{1,0:T(8,128)S(1)}, u32[]{:S(2)}, u32[]{:S(2)}) %collective-permute-start.1) | collective-permute-done | bytes 256032 | tf_op jit(solution)/shard_map/ppermute | solution.py:424
  18.0 0.2 shard_map.66
  18.3 0.1 collective-permute-start.2
  18.4 3.3 %collective-permute-start.3 = (f32[270,256]{1,0:T(8,128)S(1)}, f32[270,256]{1,0:T(8,128)S(1)}, u32[]{:S(2)}, u32[]{:S(2)}) collective-permute-start(f32[270,256]{1,0:T(8,128)S(1)} %get-tuple-element.53), channel_id=1, source_target_pairs={{1,2},{2,1},{3,4},{4,3},{5,6},{6,5},{7,8},{8,7},{9,10},{10,9},{11,... | collective-permute-start | bytes 829448 | tf_op jit(solution)/shard_map/ppermute | solution.py:424
  21.7 25.2 %all_to_all.5 = f32[256,1,128]{2,1,0:T(1,128)S(1)} all-to-all(f32[256,1,128]{2,1,0:T(1,128)S(1)} %bitcast.16), channel_id=1, replica_groups=mesh['gx'=16,'gy'=16] {'gx','gy'}, dimensions={0} | all-to-all | bytes 262144 | tf_op jit(solution)/shard_map/all_to_all | solution.py:454
  46.9 0.0 collective-permute-done.2.ya
  46.9 0.0 collective-permute-done.3.yb
  46.9 1.8 %shard_map.67 = (f32[125,6,256]{2,1,0:T(8,128)S(1)}, f32[125,6,256]{2,1,0:T(8,128)S(1)}, f32[125,6,256]{2,1,0:T(8,128)S(1)}, f32[125,6,256]{2,1,0:T(8,128)S(1)},...) custom-call(f32[125,6,256]{2,1,0:T(8,128)S(1)} %get-tuple-element.43, ...), custom_call_target="tpu_custom_call", output_to_operand_aliasing={{0}: (0, {}), {1}: (1, {}), {2}: (2, {}), {3}: (3, {})} | custom-call | bytes 9746432 | tf_op jit(solution)/shard_map/pallas_call | solution.py:403
  48.7 0.6 collective-permute-start.4
  49.3 0.7 collective-permute-start.5
  50.0 0.3 collective-permute-start.6
  50.3 1.4 %collective-permute-start.7 = (f32[150,256]{1,0:T(8,128)S(1)}, f32[150,256]{1,0:T(8,128)S(1)}, u32[]{:S(2)}, u32[]{:S(2)}) collective-permute-start(f32[150,256]{1,0:T(8,128)S(1)} %get-tuple-element.64), channel_id=1, source_target_pairs={{1,2},{2,1},{3,4},{4,3},{5,6},{6,5},{7,8},{8,7},{9,10},{10,9},{11,... | collective-permute-start | bytes 460808 | tf_op jit(solution)/shard_map/ppermute | solution.py:424
  51.7 1.2 %shard_map.68 = (f32[125,6,256]{2,1,0:T(8,128)S(1)}, f32[125,6,256]{2,1,0:T(8,128)S(1)}) custom-call(f32[125,6,256]{2,1,0:T(8,128)S(1)} %get-tuple-element.55.v, f32[125,6,256]{2,1,0:T(8,128)S(1)} %get-tuple-element.56.c0, f32[125,6,256]{2,1,0:T(8,128)S(1)} %get-tuple-element.57.c1, ...), custom_call_target="tpu_custom_call", output_to_operand_aliasing={{0}: (4, {})} | custom-call | flops 10000000 | bytes 5376000 | tf_op jit(solution)/shard_map/pallas_call | solution.py:403
  53.0 0.0 collective-permute-done.4.xa
  53.0 1.3 %collective-permute-done.5.xb = f32[150,256]{1,0:T(8,128)S(1)} collective-permute-done((f32[150,256]{1,0:T(8,128)S(1)}, f32[150,256]{1,0:T(8,128)S(1)}, u32[]{:S(2)}, u32[]{:S(2)}) %collective-permute-start.5) | collective-permute-done | bytes 153632 | tf_op jit(solution)/shard_map/ppermute | solution.py:424
  54.2 1.5 %collective-permute-done.6.ya = f32[150,256]{1,0:T(8,128)S(1)} collective-permute-done((f32[150,256]{1,0:T(8,128)S(1)}, f32[150,256]{1,0:T(8,128)S(1)}, u32[]{:S(2)}, u32[]{:S(2)}) %collective-permute-start.6) | collective-permute-done | bytes 153632 | tf_op jit(solution)/shard_map/ppermute | solution.py:424
  55.7 3.4 %collective-permute-done.7.yb = f32[150,256]{1,0:T(8,128)S(1)} collective-permute-done((f32[150,256]{1,0:T(8,128)S(1)}, f32[150,256]{1,0:T(8,128)S(1)}, u32[]{:S(2)}, u32[]{:S(2)}) %collective-permute-start.7) | collective-permute-done | bytes 153632 | tf_op jit(solution)/shard_map/ppermute | solution.py:424
  59.1 0.4 shard_map.69
  59.5 1.1 %collective-permute-start.8 = (f32[150,256]{1,0:T(8,128)S(1)}, f32[150,256]{1,0:T(8,128)S(1)}, u32[]{:S(2)}, u32[]{:S(2)}) collective-permute-start(f32[150,256]{1,0:T(8,128)S(1)} %get-tuple-element.68), channel_id=1, source_target_pairs={{0,16},{16,0},{32,48},{48,32},{64,80},{80,64},{96,112},{112,96},{1... | collective-permute-start | bytes 460808 | tf_op jit(solution)/shard_map/ppermute | solution.py:424
  60.6 0.2 collective-permute-start.9
  60.8 0.0 collective-permute-start.10
  60.8 1.5 %collective-permute-start.11 = (f32[150,256]{1,0:T(8,128)S(1)}, f32[150,256]{1,0:T(8,128)S(1)}, u32[]{:S(2)}, u32[]{:S(2)}) collective-permute-start(f32[150,256]{1,0:T(8,128)S(1)} %get-tuple-element.71), channel_id=1, source_target_pairs={{1,2},{2,1},{3,4},{4,3},{5,6},{6,5},{7,8},{8,7},{9,10},{10,9},{11,... | collective-permute-start | bytes 460808 | tf_op jit(solution)/shard_map/ppermute | solution.py:424
  62.4 1.2 %shard_map.70 = (f32[125,6,256]{2,1,0:T(8,128)S(1)}, f32[125,6,256]{2,1,0:T(8,128)S(1)}) custom-call(f32[125,6,256]{2,1,0:T(8,128)S(1)} %get-tuple-element.65.v, f32[125,6,256]{2,1,0:T(8,128)S(1)} %get-tuple-element.56.c0, f32[125,6,256]{2,1,0:T(8,128)S(1)} %get-tuple-element.57.c1, ...), custom_call_target="tpu_custom_call", output_to_operand_aliasing={{0}: (4, {})} | custom-call | flops 10000000 | bytes 5376000 | tf_op jit(solution)/shard_map/pallas_call | solution.py:403
  63.6 0.0 collective-permute-done.8.xa
  63.6 2.0 %collective-permute-done.9.xb = f32[150,256]{1,0:T(8,128)S(1)} collective-permute-done((f32[150,256]{1,0:T(8,128)S(1)}, f32[150,256]{1,0:T(8,128)S(1)}, u32[]{:S(2)}, u32[]{:S(2)}) %collective-permute-start.9) | collective-permute-done | bytes 153632 | tf_op jit(solution)/shard_map/ppermute | solution.py:424
  65.6 0.1 collective-permute-done.10.ya
  65.7 3.3 %collective-permute-done.11.yb = f32[150,256]{1,0:T(8,128)S(1)} collective-permute-done((f32[150,256]{1,0:T(8,128)S(1)}, f32[150,256]{1,0:T(8,128)S(1)}, u32[]{:S(2)}, u32[]{:S(2)}) %collective-permute-start.11) | collective-permute-done | bytes 153632 | tf_op jit(solution)/shard_map/ppermute | solution.py:424
  69.0 0.4 shard_map.71
  69.4 1.7 %collective-permute-start.12 = (f32[150,256]{1,0:T(8,128)S(1)}, f32[150,256]{1,0:T(8,128)S(1)}, u32[]{:S(2)}, u32[]{:S(2)}) collective-permute-start(f32[150,256]{1,0:T(8,128)S(1)} %get-tuple-element.76), channel_id=1, source_target_pairs={{0,16},{16,0},{32,48},{48,32},{64,80},{80,64},{96,112},{112,96},{1... | collective-permute-start | bytes 460808 | tf_op jit(solution)/shard_map/ppermute | solution.py:424
  71.1 0.5 collective-permute-start.13
  71.7 0.0 collective-permute-start.14
  71.7 1.5 %collective-permute-start.15 = (f32[150,256]{1,0:T(8,128)S(1)}, f32[150,256]{1,0:T(8,128)S(1)}, u32[]{:S(2)}, u32[]{:S(2)}) collective-permute-start(f32[150,256]{1,0:T(8,128)S(1)} %get-tuple-element.79), channel_id=1, source_target_pairs={{1,2},{2,1},{3,4},{4,3},{5,6},{6,5},{7,8},{8,7},{9,10},{10,9},{11,... | collective-permute-start | bytes 460808 | tf_op jit(solution)/shard_map/ppermute | solution.py:424
  73.2 1.2 %shard_map.72 = (f32[125,6,256]{2,1,0:T(8,128)S(1)}, f32[125,6,256]{2,1,0:T(8,128)S(1)}) custom-call(f32[125,6,256]{2,1,0:T(8,128)S(1)} %get-tuple-element.72.v, f32[125,6,256]{2,1,0:T(8,128)S(1)} %get-tuple-element.56.c0, f32[125,6,256]{2,1,0:T(8,128)S(1)} %get-tuple-element.57.c1, ...), custom_call_target="tpu_custom_call", output_to_operand_aliasing={{0}: (4, {})} | custom-call | flops 10000000 | bytes 5376000 | tf_op jit(solution)/shard_map/pallas_call | solution.py:403
  74.5 0.0 collective-permute-done.12.xa
  74.5 1.6 %collective-permute-done.13.xb = f32[150,256]{1,0:T(8,128)S(1)} collective-permute-done((f32[150,256]{1,0:T(8,128)S(1)}, f32[150,256]{1,0:T(8,128)S(1)}, u32[]{:S(2)}, u32[]{:S(2)}) %collective-permute-start.13) | collective-permute-done | bytes 153632 | tf_op jit(solution)/shard_map/ppermute | solution.py:424
  76.1 0.2 collective-permute-done.14.ya
  76.3 3.3 %collective-permute-done.15.yb = f32[150,256]{1,0:T(8,128)S(1)} collective-permute-done((f32[150,256]{1,0:T(8,128)S(1)}, f32[150,256]{1,0:T(8,128)S(1)}, u32[]{:S(2)}, u32[]{:S(2)}) %collective-permute-start.15) | collective-permute-done | bytes 153632 | tf_op jit(solution)/shard_map/ppermute | solution.py:424
  79.6 0.3 shard_map.73
  80.0 0.5 reshape.31
  80.4 1.7 %copy.26 = f32[3,2,5,5,5,1,1,256]{7,6,5,4,3,2,1,0:T(1,128)} copy(f32[3,2,5,5,5,1,1,256]{7,1,0,4,3,2,6,5:T(2,128)S(1)} %reshape.31) | data formatting | bytes 1536000 | tf_op jit(solution)/shard_map/reshape | solution.py:481
Async XLA Ops:
  3.0 1.1 %copy-start.4 = (f32[3,2,5,5,5,1,1,256]{7,6,5,4,3,2,1,0:T(1,128)S(1)}, f32[3,2,5,5,5,1,1,256]{7,6,5,4,3,2,1,0:T(1,128)}, u32[]{:S(2)}) copy-start(f32[3,2,5,5,5,1,1,256]{7,6,5,4,3,2,1,0:T(1,128)} %param.7) | copy-start | bytes 2304004
  7.0 4.9 %copy-start = (f32[3,100]{1,0:T(4,128)S(1)}, f32[3,100]{1,0:T(4,128)}, u32[]{:S(2)}) copy-start(f32[3,100]{1,0:T(4,128)} %coords.1) | copy-start | bytes 3604
  7.1 4.9 %copy-start.1 = (s32[100]{0:T(128)S(1)}, s32[100]{0:T(128)}, u32[]{:S(2)}) copy-start(s32[100]{0:T(128)} %param.8) | copy-start | bytes 1204
  7.1 4.9 %copy-start.2 = (s32[100]{0:T(128)S(1)}, s32[100]{0:T(128)}, u32[]{:S(2)}) copy-start(s32[100]{0:T(128)} %param.10) | copy-start | bytes 1204
  7.1 4.9 %copy-start.3 = (s32[100]{0:T(128)S(1)}, s32[100]{0:T(128)}, u32[]{:S(2)}) copy-start(s32[100]{0:T(128)} %param.11) | copy-start | bytes 1204
  8.6 5.0 %collective-permute-start = (f32[250,256]{1,0:T(8,128)S(1)}, f32[250,256]{1,0:T(8,128)S(1)}, u32[]{:S(2)}, u32[]{:S(2)}) collective-permute-start(f32[250,256]{1,0:T(8,128)S(1)} %get-tuple-element.48), channel_id=1, source_target_pairs={{0,16},{16,0},{32,48},{48,32},{64,80},{80,64},{96,112},{112,96},{1... | collective-permute-start | bytes 768008 | tf_op jit(solution)/shard_map/ppermute | solution.py:424
  11.9 6.1 %collective-permute-start.1 = (f32[250,256]{1,0:T(8,128)S(1)}, f32[250,256]{1,0:T(8,128)S(1)}, u32[]{:S(2)}, u32[]{:S(2)}) collective-permute-start(f32[250,256]{1,0:T(8,128)S(1)} %get-tuple-element.49), channel_id=1, source_target_pairs={{16,32},{32,16},{48,64},{64,48},{80,96},{96,80},{112,128},{128,112... | collective-permute-start | bytes 768008 | tf_op jit(solution)/shard_map/ppermute | solution.py:424
  18.3 28.7 %collective-permute-start.2 = (f32[270,256]{1,0:T(8,128)S(1)}, f32[270,256]{1,0:T(8,128)S(1)}, u32[]{:S(2)}, u32[]{:S(2)}) collective-permute-start(f32[270,256]{1,0:T(8,128)S(1)} %get-tuple-element.52), channel_id=1, source_target_pairs={{0,1},{1,0},{2,3},{3,2},{4,5},{5,4},{6,7},{7,6},{8,9},{9,8},{10,11... | collective-permute-start | bytes 829448 | tf_op jit(solution)/shard_map/ppermute | solution.py:424
  18.4 28.6 %collective-permute-start.3 = (f32[270,256]{1,0:T(8,128)S(1)}, f32[270,256]{1,0:T(8,128)S(1)}, u32[]{:S(2)}, u32[]{:S(2)}) collective-permute-start(f32[270,256]{1,0:T(8,128)S(1)} %get-tuple-element.53), channel_id=1, source_target_pairs={{1,2},{2,1},{3,4},{4,3},{5,6},{6,5},{7,8},{8,7},{9,10},{10,9},{11,... | collective-permute-start | bytes 829448 | tf_op jit(solution)/shard_map/ppermute | solution.py:424
  48.7 4.3 %collective-permute-start.4 = (f32[150,256]{1,0:T(8,128)S(1)}, f32[150,256]{1,0:T(8,128)S(1)}, u32[]{:S(2)}, u32[]{:S(2)}) collective-permute-start(f32[150,256]{1,0:T(8,128)S(1)} %get-tuple-element.61), channel_id=1, source_target_pairs={{0,16},{16,0},{32,48},{48,32},{64,80},{80,64},{96,112},{112,96},{1... | collective-permute-start | bytes 460808 | tf_op jit(solution)/shard_map/ppermute | solution.py:424
  49.3 5.0 %collective-permute-start.5 = (f32[150,256]{1,0:T(8,128)S(1)}, f32[150,256]{1,0:T(8,128)S(1)}, u32[]{:S(2)}, u32[]{:S(2)}) collective-permute-start(f32[150,256]{1,0:T(8,128)S(1)} %get-tuple-element.62), channel_id=1, source_target_pairs={{16,32},{32,16},{48,64},{64,48},{80,96},{96,80},{112,128},{128,112... | collective-permute-start | bytes 460808 | tf_op jit(solution)/shard_map/ppermute | solution.py:424
  50.0 5.7 %collective-permute-start.6 = (f32[150,256]{1,0:T(8,128)S(1)}, f32[150,256]{1,0:T(8,128)S(1)}, u32[]{:S(2)}, u32[]{:S(2)}) collective-permute-start(f32[150,256]{1,0:T(8,128)S(1)} %get-tuple-element.63), channel_id=1, source_target_pairs={{0,1},{1,0},{2,3},{3,2},{4,5},{5,4},{6,7},{7,6},{8,9},{9,8},{10,11... | collective-permute-start | bytes 460808 | tf_op jit(solution)/shard_map/ppermute | solution.py:424
  50.3 8.7 %collective-permute-start.7 = (f32[150,256]{1,0:T(8,128)S(1)}, f32[150,256]{1,0:T(8,128)S(1)}, u32[]{:S(2)}, u32[]{:S(2)}) collective-permute-start(f32[150,256]{1,0:T(8,128)S(1)} %get-tuple-element.64), channel_id=1, source_target_pairs={{1,2},{2,1},{3,4},{4,3},{5,6},{6,5},{7,8},{8,7},{9,10},{10,9},{11,... | collective-permute-start | bytes 460808 | tf_op jit(solution)/shard_map/ppermute | solution.py:424
  59.5 4.1 %collective-permute-start.8 = (f32[150,256]{1,0:T(8,128)S(1)}, f32[150,256]{1,0:T(8,128)S(1)}, u32[]{:S(2)}, u32[]{:S(2)}) collective-permute-start(f32[150,256]{1,0:T(8,128)S(1)} %get-tuple-element.68), channel_id=1, source_target_pairs={{0,16},{16,0},{32,48},{48,32},{64,80},{80,64},{96,112},{112,96},{1... | collective-permute-start | bytes 460808 | tf_op jit(solution)/shard_map/ppermute | solution.py:424
  60.6 5.0 %collective-permute-start.9 = (f32[150,256]{1,0:T(8,128)S(1)}, f32[150,256]{1,0:T(8,128)S(1)}, u32[]{:S(2)}, u32[]{:S(2)}) collective-permute-start(f32[150,256]{1,0:T(8,128)S(1)} %get-tuple-element.69), channel_id=1, source_target_pairs={{16,32},{32,16},{48,64},{64,48},{80,96},{96,80},{112,128},{128,112... | collective-permute-start | bytes 460808 | tf_op jit(solution)/shard_map/ppermute | solution.py:424
  60.8 4.8 %collective-permute-start.10 = (f32[150,256]{1,0:T(8,128)S(1)}, f32[150,256]{1,0:T(8,128)S(1)}, u32[]{:S(2)}, u32[]{:S(2)}) collective-permute-start(f32[150,256]{1,0:T(8,128)S(1)} %get-tuple-element.70), channel_id=1, source_target_pairs={{0,1},{1,0},{2,3},{3,2},{4,5},{5,4},{6,7},{7,6},{8,9},{9,8},{10,11... | collective-permute-start | bytes 460808 | tf_op jit(solution)/shard_map/ppermute | solution.py:424
  60.8 8.1 %collective-permute-start.11 = (f32[150,256]{1,0:T(8,128)S(1)}, f32[150,256]{1,0:T(8,128)S(1)}, u32[]{:S(2)}, u32[]{:S(2)}) collective-permute-start(f32[150,256]{1,0:T(8,128)S(1)} %get-tuple-element.71), channel_id=1, source_target_pairs={{1,2},{2,1},{3,4},{4,3},{5,6},{6,5},{7,8},{8,7},{9,10},{10,9},{11,... | collective-permute-start | bytes 460808 | tf_op jit(solution)/shard_map/ppermute | solution.py:424
  69.4 5.0 %collective-permute-start.12 = (f32[150,256]{1,0:T(8,128)S(1)}, f32[150,256]{1,0:T(8,128)S(1)}, u32[]{:S(2)}, u32[]{:S(2)}) collective-permute-start(f32[150,256]{1,0:T(8,128)S(1)} %get-tuple-element.76), channel_id=1, source_target_pairs={{0,16},{16,0},{32,48},{48,32},{64,80},{80,64},{96,112},{112,96},{1... | collective-permute-start | bytes 460808 | tf_op jit(solution)/shard_map/ppermute | solution.py:424
  71.1 5.0 %collective-permute-start.13 = (f32[150,256]{1,0:T(8,128)S(1)}, f32[150,256]{1,0:T(8,128)S(1)}, u32[]{:S(2)}, u32[]{:S(2)}) collective-permute-start(f32[150,256]{1,0:T(8,128)S(1)} %get-tuple-element.77), channel_id=1, source_target_pairs={{16,32},{32,16},{48,64},{64,48},{80,96},{96,80},{112,128},{128,112... | collective-permute-start | bytes 460808 | tf_op jit(solution)/shard_map/ppermute | solution.py:424
  71.7 4.6 %collective-permute-start.14 = (f32[150,256]{1,0:T(8,128)S(1)}, f32[150,256]{1,0:T(8,128)S(1)}, u32[]{:S(2)}, u32[]{:S(2)}) collective-permute-start(f32[150,256]{1,0:T(8,128)S(1)} %get-tuple-element.78), channel_id=1, source_target_pairs={{0,1},{1,0},{2,3},{3,2},{4,5},{5,4},{6,7},{7,6},{8,9},{9,8},{10,11... | collective-permute-start | bytes 460808 | tf_op jit(solution)/shard_map/ppermute | solution.py:424
  71.7 7.9 %collective-permute-start.15 = (f32[150,256]{1,0:T(8,128)S(1)}, f32[150,256]{1,0:T(8,128)S(1)}, u32[]{:S(2)}, u32[]{:S(2)}) collective-permute-start(f32[150,256]{1,0:T(8,128)S(1)} %get-tuple-element.79), channel_id=1, source_target_pairs={{1,2},{2,1},{3,4},{4,3},{5,6},{6,5},{7,8},{8,7},{9,10},{10,9},{11,... | collective-permute-start | bytes 460808 | tf_op jit(solution)/shard_map/ppermute | solution.py:424
where the time goes:
time: 82.3 us; the launch traced here: 82.1 us
  blocking collectives  25.2 us (31%)
  waiting for transfers between devices  21.1 us (26%)
  starting transfers between devices  16.4 us (20%)
  Pallas kernels  10 us (12%)
  other arithmetic  4.83 us (6%)
  local copies, waits for them, and re-layouts  4.32 us (5%)
    all_to_all x1, blocking collectives, body(): lax.all_to_all(table.reshape(devices, 1, 128), ('gx', 'gy'), 0, 0)  25.2 us
    ppermute x16, waiting for transfers between devices, swap(): return lax.ppermute(x, axis, pairs(lax.axis_size(axis), offset))  21.1 us
    ppermute x16, starting transfers between devices, swap(): return lax.ppermute(x, axis, pairs(lax.axis_size(axis), offset))  16.4 us
    pallas_call x10, Pallas kernels, call(): pl.pallas_call(kernel, out_shape=[jax.ShapeDtypeStruct(s, f32) for s in o...  10 us
    unnamed x2, other arithmetic  4.83 us
    reshape x2, local copies, waits for them, and re-layouts, body(): return jnp.transpose(out, (1, 0, 2)).reshape(velocity.shape)  2.12 us
  transfers between devices with their start and end apart: 16, of which 10 were waited for; matrix products, arithmetic and copies ran while one was open for 0% of the time, Pallas kernels for 6%

commit v1 on v0

--- a/solution.py
+++ b/solution.py
@@ -101,9 +101,7 @@
     ref[ij * NP + 4] = high + pltpu.roll(low, EZ - 1, 1)
 
 
-def first_kernel(vel, conv, u8, c0, c1, c2, w, xa, xb):
-    a, b, n, m, ea, eb, ia, ja, sx, sy = place()
-    lane, odd_row = lane_index(), row_index() % 2 == 1
+def face_scale(lane, a, b, n, m):
     hx = {0: jnp.where(a > 0, 0.5, 1.0), 4: jnp.where(a < n - 1, 0.5, 1.0)}
     hy = {0: jnp.where(b > 0, 0.5, 1.0), 4: jnp.where(b < m - 1, 0.5, 1.0)}
     one = jnp.full((ROWS, EZ), -1.0, f32)
@@ -111,45 +109,108 @@
         0: jnp.where(lane == 0, 0.0, -0.5).astype(f32),
         4: jnp.where(lane == EZ - 1, 0.0, -0.5).astype(f32),
     }
-    for i in range(NP):
-        for j in range(NP):
-            side = hx.get(i, 1.0) * hy.get(j, 1.0)
+
+    def scale(i, j, k):
+        side = hx.get(i, 1.0) * hy.get(j, 1.0)
+        out = hz.get(k, one)
+        return out * side.astype(f32) if i in hx or j in hy else out
+
+    return scale
+
+
+def pinned_line(u, lane):
+    u[0] = jnp.where(lane == 0, 0.0, u[0])
+    u[4] = jnp.where(lane == EZ - 1, 0.0, u[4])
+    return u
+
+
+def row_copies(src, dst, sem, first, count):
+    return [
+        pltpu.make_async_copy(
+            src.at[r, pl.ds(first, count), 0, :], dst.at[pl.ds(first, count), r, :], sem.at[r]
+        )
+        for r in range(ROWS)
+    ]
+
+
+def opening_kernel(vel, conv, u8, xa, xb, cbuf, sem):
+    a, b, n, m, ea, eb, ia, ja, sx, sy = place()
+    copies = row_copies(vel, u8, sem.at[0], 0, PTS)
+    faces = row_copies(conv, cbuf, sem.at[1], 0, 25) + row_copies(conv, cbuf, sem.at[2], 100, 25)
+    for c in copies + faces:
+        c.start()
+    lane, odd_row = lane_index(), row_index() % 2 == 1
+    scale = face_scale(lane, a, b, n, m)
+    for c in copies + faces:
+        c.wait()
+    done = {}
+    for i in (0, 4):
+        gs, gt = {}, {}
+        for k in range(NP):
+            line = line_derivative([u8[pt(i, j, k), 0:ROWS] for j in range(NP)])
+            for j in range(NP):
+                gs[j, k] = line[j]
+        for j in range(NP):
+            line = line_derivative(pinned_line([u8[pt(i, j, k), 0:ROWS] for k in range(NP)], lane))
+            for k in range(NP):
+                gt[j, k] = line[k]
+        for j in range(NP):
+            for k in range(NP):
+                cc = cbuf[pt(i, j, k), 0:ROWS] * scale(i, j, k)
+                ends = end_derivatives([u8[pt(q, j, k), 0:ROWS] for q in range(NP)])
+                w = (
+                    widen(cc[0:2], odd_row) * ends[i // 4]
+                    + widen(cc[2:4], odd_row) * gs[j, k]
+                    + widen(cc[4:6], odd_row) * gt[j, k]
+                )
+                r = (j * NP + k) * 10
+                if i == 0:
+                    xa[r : r + 6], xa[r + 6 : r + 10] = w, cc[2:6]
+                else:
+                    low, clow = xa[r : r + 6], xa[r + 6 : r + 10]
+                    xa[r : r + 6] = jnp.where(ea, w, low)
+                    xa[r + 6 : r + 10] = jnp.where(ea, cc[2:6], clow)
+                    xb[r : r + 6] = jnp.where(ea, low, w) * sx
+                    xb[r + 6 : r + 10] = jnp.where(ea, clow, cc[2:6]) * sx
+
+
+def coefficients(u8, cbuf, c0, c1, c2, w):
+    a, b, n, m, ea, eb, ia, ja, sx, sy = place()
+    lane, odd_row = lane_index(), row_index() % 2 == 1
+    scale = face_scale(lane, a, b, n, m)
+    for i in range(NP):
+        for j in range(NP):
             for k in range(NP):
                 p = pt(i, j, k)
-                scale = hz.get(k, one)
-                if i in hx or j in hy:
-                    scale = scale * side.astype(f32)
-                cc = conv[p] * scale
+                cc = cbuf[p, 0:ROWS] * scale(i, j, k)
                 c0[p] = widen(cc[0:2], odd_row)
                 c1[p] = widen(cc[2:4], odd_row)
                 c2[p] = widen(cc[4:6], odd_row)
-                u8[p, 0:ROWS] = vel[p]
     for j in range(NP):
         for k in range(NP):
-            g = line_derivative([vel[pt(i, j, k)] for i in range(NP)])
+            g = line_derivative([u8[pt(i, j, k), 0:ROWS] for i in range(NP)])
             for i in range(NP):
                 w[pt(i, j, k)] = c0[pt(i, j, k)] * g[i]
     for i in range(NP):
         for k in range(NP):
-            g = line_derivative([vel[pt(i, j, k)] for j in range(NP)])
+            g = line_derivative([u8[pt(i, j, k), 0:ROWS] for j in range(NP)])
             for j in range(NP):
                 w[pt(i, j, k)] += c1[pt(i, j, k)] * g[j]
     for i in range(NP):
         for j in range(NP):
-            u = [vel[pt(i, j, k)] for k in range(NP)]
-            u[0] = jnp.where(lane == 0, 0.0, u[0])
-            u[4] = jnp.where(lane == EZ - 1, 0.0, u[4])
-            g = line_derivative(u)
+            g = line_derivative(pinned_line([u8[pt(i, j, k), 0:ROWS] for k in range(NP)], lane))
             for k in range(NP):
                 w[pt(i, j, k)] += c2[pt(i, j, k)] * g[k]
-    for jk in range(NP * NP):
-        pa, pb = ia * 25 + jk, (4 - ia) * 25 + jk
-        xa[jk * 10 : jk * 10 + 6] = w[pa]
-        xa[jk * 10 + 6 : jk * 10 + 8] = c1[pa, 0:2]
-        xa[jk * 10 + 8 : jk * 10 + 10] = c2[pa, 0:2]
-        xb[jk * 10 : jk * 10 + 6] = w[pb] * sx
-        xb[jk * 10 + 6 : jk * 10 + 8] = c1[pb, 0:2] * sx
-        xb[jk * 10 + 8 : jk * 10 + 10] = c2[pb, 0:2] * sx
+
+
+def query_kernel(u8, conv, donor, coords, dest, target, table, c0, c1, c2, w, cbuf, sem):
+    copies = row_copies(conv, cbuf, sem, 0, PTS)
+    for c in copies:
+        c.start()
+    make_table(u8, donor, coords, dest, target, table)
+    for c in copies:
+        c.wait()
+    coefficients(u8, cbuf, c0, c1, c2, w)
 
 
 def second_kernel(w, c0, c2, xa, xb, ya, yb):
@@ -181,7 +242,7 @@
                 dst[r : r + 2] = put(edge(j_even, k, 8, 10, low_side))
 
 
-def query_kernel(u8, donor, coords, dest, target, table):
+def make_table(u8, donor, coords, dest, target, table):
     queries = donor.shape[1]
     devices = table.shape[0]
     n, m = lax.axis_size("gx"), lax.axis_size("gy")
@@ -249,7 +310,7 @@
     table[...] = jnp.concatenate(slots, axis=0).T
 
 
-def third_kernel(w_in, c0_in, c1_in, c2_in, u8, xa, xb, ya, yb, table, v, c0, c1, c2, acc, oxa, oxb, oya, oyb, z):
+def third_kernel(w_in, c0_in, c1_in, c2_in, u8, xa, xb, ya, yb, table, v, c0, c1, c2, acc, oya, oyb, z):
     a, b, n, m, ea, eb, ia, ja, sx, sy = place()
     del w_in, c0_in, c1_in, c2_in
     lane, row = lane_index(), row_index()
@@ -325,10 +386,10 @@
         z_sum(v, ij)
         z_sum(c0, ij)
         z_sum(c1, ij)
-    messages(v, c0, c1, oxa, oxb, oya, oyb)
-
-
-def messages(v, c0, c1, oxa, oxb, oya, oyb):
+    second_messages(v, c1, oya, oyb)
+
+
+def second_messages(v, c1, oya, oyb):
     a, b, n, m, ea, eb, ia, ja, sx, sy = place()
     for i in range(NP):
         for k in range(NP):
@@ -337,6 +398,10 @@
             r = (i * NP + k) * 6
             oya[r : r + 6] = jnp.where(eb, high, low)
             oyb[r : r + 6] = jnp.where(eb, low, high) * sy
+
+
+def first_messages(v, c0, oxa, oxb):
+    a, b, n, m, ea, eb, ia, ja, sx, sy = place()
     for j in range(NP):
         for k in range(NP):
             low, high = end_derivatives([v[pt(i, j, k)] for i in range(NP)])
@@ -358,10 +423,10 @@
                 v[i * 25 + face * NP + k] += src[r : r + 6]
 
 
-def send_kernel(w_in, c0, c1, xa, xb, ya, yb, v, oxa, oxb, oya, oyb):
+def send_kernel(w_in, c1, xa, xb, ya, yb, v, oya, oyb):
     del w_in
     take_messages(v, xa, xb, ya, yb)
-    messages(v, c0, c1, oxa, oxb, oya, oyb)
+    second_messages(v, c1, oya, oyb)
 
 
 def local_kernel(coef, v, c0, c1, c2, acc_in, acc, w):
@@ -388,23 +453,36 @@
                 w[pt(i, j, k)] += t[k]
 
 
-def last_kernel(coef, w_in, acc, xa, xb, ya, yb, v, out):
+def last_kernel(coef, w_in, acc, xa, xb, ya, yb, v, out, obuf, sem):
     del w_in
     take_messages(v, xa, xb, ya, yb)
-    for p in range(PTS):
-        out[p] = acc[p] + v[p] * coef
+    started = []
+    for i in range(NP):
+        for p in range(i * 25, i * 25 + 25):
+            obuf[p, 0:ROWS] = acc[p] + v[p] * coef
+        for r in range(ROWS):
+            rows = pl.ds(i * 25, 25)
+            c = pltpu.make_async_copy(obuf.at[rows, r, :], out.at[r, rows, 0, :], sem.at[i, r])
+            c.start()
+            started.append(c)
+    for c in started:
+        c.wait()
 
 
 FIELD = (PTS, ROWS, EZ)
+
+
+RAW = (ROWS, PTS, 1, EZ)
 
 
 def call(kernel, outs, args, aliases=None, scratch=(), flops=0):
     moved = sum(4 * math.prod(x.shape) for x in args) + sum(4 * math.prod(s) for s in outs)
+    spec = lambda shape: pl.BlockSpec(memory_space=pl.ANY if shape == RAW else pltpu.VMEM)
     return pl.pallas_call(
         kernel,
         out_shape=[jax.ShapeDtypeStruct(s, f32) for s in outs],
-        in_specs=[pl.BlockSpec(memory_space=pltpu.VMEM)] * len(args),
-        out_specs=[pl.BlockSpec(memory_space=pltpu.VMEM)] * len(outs),
+        in_specs=[spec(x.shape) for x in args],
+        out_specs=[spec(s) for s in outs],
         input_output_aliases=aliases or {},
         scratch_shapes=list(scratch),
         compiler_params=pltpu.CompilerParams(vmem_limit_bytes=24 * 1024 * 1024),
@@ -431,30 +509,35 @@
 def body(velocity, convecting, donor_element, coords, dest_rank, target):
     devices = lax.axis_size("gx") * lax.axis_size("gy")
     queries = dest_rank.shape[0]
-    vel = jnp.transpose(velocity.reshape(ROWS, PTS, EZ), (1, 0, 2))
-    conv = jnp.transpose(convecting.reshape(ROWS, PTS, EZ), (1, 0, 2))
-    u8, c0, c1, c2, w, xa, xb = call(
-        first_kernel, [(PTS, 8, EZ)] + [FIELD] * 4 + [(250, EZ)] * 2, [vel, conv]
+    vel, conv = velocity.reshape(RAW), convecting.reshape(RAW)
+    whole = pltpu.VMEM((PTS, 8, EZ), f32)
+    u8, xa, xb = call(
+        opening_kernel,
+        [(PTS, 8, EZ)] + [(250, EZ)] * 2,
+        [vel, conv],
+        scratch=[whole, pltpu.SemaphoreType.DMA((3, ROWS))],
     )
     xa, xb = swap(xa, "gx", 0), swap(xb, "gx", 1)
-    (table,) = call(
+    table, c0, c1, c2, w = call(
         query_kernel,
-        [(devices, 128)],
+        [(devices, 128)] + [FIELD] * 4,
         [
             u8,
+            conv,
             donor_element.reshape(1, queries),
             coords,
             dest_rank.reshape(1, queries),
             target.reshape(1, queries),
         ],
+        scratch=[whole, pltpu.SemaphoreType.DMA((ROWS,))],
     )
     ya, yb = call(second_kernel, [(270, EZ)] * 2, [w, c0, c2, xa, xb])
     table, ya, yb = lax.optimization_barrier((table, ya, yb))
     ya, yb = swap(ya, "gy", 0), swap(yb, "gy", 1)
     table = lax.all_to_all(table.reshape(devices, 1, 128), ("gx", "gy"), 0, 0).reshape(devices, 128)
-    v, c0, c1, c2, acc, oxa, oxb, oya, oyb = call(
+    v, c0, c1, c2, acc, ya, yb = call(
         third_kernel,
-        [FIELD] * 5 + [(150, EZ)] * 4,
+        [FIELD] * 5 + [(150, EZ)] * 2,
         [w, c0, c1, c2, u8, xa, xb, ya, yb, table],
         aliases={0: 0, 1: 1, 2: 2, 3: 3},
         scratch=[pltpu.VMEM((49, ROWS, EZ), f32)],
@@ -462,7 +545,9 @@
     coef = 1.0
     for stage in range(1, 4):
         coef = coef * time_step / stage
-        got = swap_all(oxa, oxb, oya, oyb)
+        ya, yb = swap(ya, "gy", 0), swap(yb, "gy", 1)
+        xa, xb = call(first_messages, [(150, EZ)] * 2, [v, c0])
+        got = [swap(xa, "gx", 0), swap(xb, "gx", 1), ya, yb]
         acc, w = call(
             functools.partial(local_kernel, coef),
             [FIELD] * 2,
@@ -471,14 +556,18 @@
             flops=10**7,
         )
         if stage < 3:
-            v, oxa, oxb, oya, oyb = call(
-                send_kernel, [FIELD] + [(150, EZ)] * 4, [w, c0, c1, *got], aliases={0: 0}
+            v, ya, yb = call(
+                send_kernel, [FIELD] + [(150, EZ)] * 2, [w, c1, *got], aliases={0: 0}
             )
     coef = coef * time_step / 4
     _, out = call(
-        functools.partial(last_kernel, coef), [FIELD] * 2, [w, acc, *got], aliases={0: 0}
-    )
-    return jnp.transpose(out, (1, 0, 2)).reshape(velocity.shape)
+        functools.partial(last_kernel, coef),
+        [FIELD, RAW],
+        [w, acc, *got],
+        aliases={0: 0},
+        scratch=[whole, pltpu.SemaphoreType.DMA((NP, ROWS))],
+    )
+    return out.reshape(velocity.shape)
 
 
 def solution(mesh):

time: 82.3 us -> 73.2 us (0.89)
  waiting for transfers between devices: 21.1 us -> 12.5 us
  other arithmetic: 4.83 us -> 0 us
  Pallas kernels: 10 us -> 12.9 us
  starting transfers between devices: 16.4 us -> 19.2 us
  local copies, waits for them, and re-layouts: 4.32 us -> 2.94 us
    ppermute x16, waiting for transfers between devices: 21.1 us -> 12.5 us  [swap(): return lax.ppermute(x, axis, pairs(lax.axis_size(axis), offset))]
    unnamed x2 -> x0, other arithmetic: 4.83 us -> none
    pallas_call x10 -> x13, Pallas kernels: 10 us -> 12.9 us  [call(): pl.pallas_call(kernel, out_shape=[jax.ShapeDtypeStruct(s, f32) for s in o...]
    ppermute x16, starting transfers between devices: 16.4 us -> 19.2 us  [swap(): return lax.ppermute(x, axis, pairs(lax.axis_size(axis), offset))]
    reshape x4 -> x0, local copies, waits for them, and re-layouts: 2.39 us -> none  [the longest x2 2.12 us: body(): return jnp.transpose(out, (1, 0, 2)).reshape(velocity.shape)]
    unnamed x10 -> x12, local copies, waits for them, and re-layouts: 1 us -> 2.94 us
    transpose x1 -> x0, local copies, waits for them, and re-layouts: 0.93 us -> none  [body(): conv = jnp.transpose(convecting.reshape(ROWS, PTS, EZ), (1, 0, 2))]
  transfers between devices with their start and end apart: 16 -> 16, of which waited for: 10 -> 6; matrix products, arithmetic and copies ran while one was open for 0% -> 0% of each run, Pallas kernels for 6% -> 10%
where the time goes in v1:
time: 73.2 us; the launch traced here: 73 us
  blocking collectives  25.2 us (34%)
  starting transfers between devices  19.2 us (26%)
  Pallas kernels  12.9 us (18%)
  waiting for transfers between devices  12.5 us (17%)
  local copies, waits for them, and re-layouts  2.94 us (4%)
    all_to_all x1, blocking collectives, body(): lax.all_to_all(table.reshape(devices, 1, 128), ('gx', 'gy'), 0, 0)  25.2 us
    ppermute x16, starting transfers between devices, swap(): return lax.ppermute(x, axis, pairs(lax.axis_size(axis), offset))  19.2 us
    pallas_call x13, Pallas kernels, call(): pl.pallas_call(kernel, out_shape=[jax.ShapeDtypeStruct(s, f32) for s in o...  12.9 us
    ppermute x16, waiting for transfers between devices, swap(): return lax.ppermute(x, axis, pairs(lax.axis_size(axis), offset))  12.5 us
    unnamed x12, local copies, waits for them, and re-layouts  2.94 us
  transfers between devices with their start and end apart: 16, of which 6 were waited for; matrix products, arithmetic and copies ran while one was open for 0% of the time, Pallas kernels for 10%

profile of v1, /device:TPU:1, one launch (start us, length us, event | category | flops | bytes accessed | tf_op | source)
XLA Modules:
  0.0 73.0 jit_solution(6726298897617961603)
XLA Ops:
  0.0 0.0 copy-start
  0.0 1.1 %copy-done = f32[3,2,5,5,5,1,1,256]{7,6,5,4,3,2,1,0:T(1,128)S(1)} copy-done((f32[3,2,5,5,5,1,1,256]{7,6,5,4,3,2,1,0:T(1,128)S(1)}, f32[3,2,5,5,5,1,1,256]{7,6,5,4,3,2,1,0:T(1,128)}, u32[]{:S(2)}) %copy-start) | copy-done | bytes 768024
  1.1 0.0 copy-start.1
  1.1 1.1 %copy-done.1 = f32[3,2,5,5,5,1,1,256]{7,6,5,4,3,2,1,0:T(1,128)S(1)} copy-done((f32[3,2,5,5,5,1,1,256]{7,6,5,4,3,2,1,0:T(1,128)S(1)}, f32[3,2,5,5,5,1,1,256]{7,6,5,4,3,2,1,0:T(1,128)}, u32[]{:S(2)}) %copy-start.1) | copy-done | bytes 768024
  2.3 1.6 %shard_map.64 = (f32[125,8,256]{2,1,0:T(8,128)S(1)}, f32[250,256]{1,0:T(8,128)S(1)}, f32[250,256]{1,0:T(8,128)S(1)}) custom-call(f32[6,125,1,256]{3,2,1,0:T(1,128)S(1)} %bitcast.14, f32[6,125,1,256]{3,2,1,0:T(1,128)S(1)} %bitcast.12), custom_call_target="tpu_custom_call" | custom-call | bytes 3072000 | tf_op jit(solution)/shard_map/pallas_call | solution.py:481
  3.9 3.3 %collective-permute-start = (f32[250,256]{1,0:T(8,128)S(1)}, f32[250,256]{1,0:T(8,128)S(1)}, u32[]{:S(2)}, u32[]{:S(2)}) collective-permute-start(f32[250,256]{1,0:T(8,128)S(1)} %get-tuple-element.49), channel_id=1, source_target_pairs={{0,16},{16,0},{32,48},{48,32},{64,80},{80,64},{96,112},{112,96},{1... | collective-permute-start | bytes 768008 | tf_op jit(solution)/shard_map/ppermute | solution.py:502
  7.2 0.0 collective-permute-start.1
  7.2 0.0 copy-start.2
  7.2 0.0 copy-start.3
  7.2 0.0 copy-start.4
  7.2 0.0 copy-start.5
  7.2 0.7 copy-done.2
  7.9 0.0 copy-done.3
  7.9 0.0 copy-done.4
  7.9 0.0 copy-done.5
  7.9 3.5 %shard_map.65 = (f32[256,128]{1,0:T(8,128)S(1)}, f32[125,6,256]{2,1,0:T(8,128)S(1)}, f32[125,6,256]{2,1,0:T(8,128)S(1)}, f32[125,6,256]{2,1,0:T(8,128)S(1)}, f32[125,6,256]{2,1,0:T(8,128)S(1)}) custom-call(f32[125,8,256]{2,1,0:T(8,128)S(1)} %get-tuple-element.44.u8, f32[6,125,1,256]{3,2,1,0:T(1,128)S(1)} %bitcast.13, s32[1,100]{1,0:T(1,128)S(1)} %bitcast.17, ...), custom_call_target="tpu_custom_call" | custom-call | bytes 4997472 | tf_op jit(solution)/shard_map/pallas_call | solution.py:481
  11.4 0.0 collective-permute-done.xa
  11.4 1.9 %collective-permute-done.1.xb = f32[250,256]{1,0:T(8,128)S(1)} collective-permute-done((f32[250,256]{1,0:T(8,128)S(1)}, f32[250,256]{1,0:T(8,128)S(1)}, u32[]{:S(2)}, u32[]{:S(2)}) %collective-permute-start.1) | collective-permute-done | bytes 256032 | tf_op jit(solution)/shard_map/ppermute | solution.py:502
  13.3 0.2 shard_map.66
  13.5 0.1 collective-permute-start.2
  13.6 3.4 %collective-permute-start.3 = (f32[270,256]{1,0:T(8,128)S(1)}, f32[270,256]{1,0:T(8,128)S(1)}, u32[]{:S(2)}, u32[]{:S(2)}) collective-permute-start(f32[270,256]{1,0:T(8,128)S(1)} %get-tuple-element.55), channel_id=1, source_target_pairs={{1,2},{2,1},{3,4},{4,3},{5,6},{6,5},{7,8},{8,7},{9,10},{10,9},{11,... | collective-permute-start | bytes 829448 | tf_op jit(solution)/shard_map/ppermute | solution.py:502
  17.0 25.2 %all_to_all.5 = f32[256,1,128]{2,1,0:T(1,128)S(1)} all-to-all(f32[256,1,128]{2,1,0:T(1,128)S(1)} %bitcast.16), channel_id=1, replica_groups=mesh['gx'=16,'gy'=16] {'gx','gy'}, dimensions={0} | all-to-all | bytes 262144 | tf_op jit(solution)/shard_map/all_to_all | solution.py:537
  42.1 0.0 collective-permute-done.2.ya
  42.1 0.0 collective-permute-done.3.yb
  42.1 1.6 %shard_map.67 = (f32[125,6,256]{2,1,0:T(8,128)S(1)}, f32[125,6,256]{2,1,0:T(8,128)S(1)}, f32[125,6,256]{2,1,0:T(8,128)S(1)}, f32[125,6,256]{2,1,0:T(8,128)S(1)},...) custom-call(f32[125,6,256]{2,1,0:T(8,128)S(1)} %get-tuple-element.45, ...), custom_call_target="tpu_custom_call", output_to_operand_aliasing={{0}: (0, {}), {1}: (1, {}), {2}: (2, {}), {3}: (3, {})} | custom-call | bytes 9439232 | tf_op jit(solution)/shard_map/pallas_call | solution.py:481
  43.7 0.4 collective-permute-start.6
  44.1 0.8 %collective-permute-start.7 = (f32[150,256]{1,0:T(8,128)S(1)}, f32[150,256]{1,0:T(8,128)S(1)}, u32[]{:S(2)}, u32[]{:S(2)}) collective-permute-start(f32[150,256]{1,0:T(8,128)S(1)} %get-tuple-element.66), channel_id=1, source_target_pairs={{1,2},{2,1},{3,4},{4,3},{5,6},{6,5},{7,8},{8,7},{9,10},{10,9},{11,... | collective-permute-start | bytes 460808 | tf_op jit(solution)/shard_map/ppermute | solution.py:502
  44.9 0.2 shard_map.69
  45.1 1.8 %collective-permute-start.4 = (f32[150,256]{1,0:T(8,128)S(1)}, f32[150,256]{1,0:T(8,128)S(1)}, u32[]{:S(2)}, u32[]{:S(2)}) collective-permute-start(f32[150,256]{1,0:T(8,128)S(1)} %get-tuple-element.63), channel_id=1, source_target_pairs={{0,16},{16,0},{32,48},{48,32},{64,80},{80,64},{96,112},{112,96},{1... | collective-permute-start | bytes 460808 | tf_op jit(solution)/shard_map/ppermute | solution.py:502
  46.9 0.8 %collective-permute-start.5 = (f32[150,256]{1,0:T(8,128)S(1)}, f32[150,256]{1,0:T(8,128)S(1)}, u32[]{:S(2)}, u32[]{:S(2)}) collective-permute-start(f32[150,256]{1,0:T(8,128)S(1)} %get-tuple-element.64), channel_id=1, source_target_pairs={{16,32},{32,16},{48,64},{64,48},{80,96},{96,80},{112,128},{128,112... | collective-permute-start | bytes 460808 | tf_op jit(solution)/shard_map/ppermute | solution.py:502
  47.7 1.2 %shard_map.68 = (f32[125,6,256]{2,1,0:T(8,128)S(1)}, f32[125,6,256]{2,1,0:T(8,128)S(1)}) custom-call(f32[125,6,256]{2,1,0:T(8,128)S(1)} %get-tuple-element.57.v, f32[125,6,256]{2,1,0:T(8,128)S(1)} %get-tuple-element.58.c0, f32[125,6,256]{2,1,0:T(8,128)S(1)} %get-tuple-element.59.c1, ...), custom_call_target="tpu_custom_call", output_to_operand_aliasing={{0}: (4, {})} | custom-call | flops 10000000 | bytes 5376000 | tf_op jit(solution)/shard_map/pallas_call | solution.py:481
  49.0 0.0 collective-permute-done.6.ya
  49.0 3.2 %collective-permute-done.7.yb = f32[150,256]{1,0:T(8,128)S(1)} collective-permute-done((f32[150,256]{1,0:T(8,128)S(1)}, f32[150,256]{1,0:T(8,128)S(1)}, u32[]{:S(2)}, u32[]{:S(2)}) %collective-permute-start.7) | collective-permute-done | bytes 153632 | tf_op jit(solution)/shard_map/ppermute | solution.py:502
  52.2 0.0 collective-permute-done.4.xa
  52.2 0.0 collective-permute-done.5.xb
  52.2 0.3 shard_map.70
  52.5 0.1 collective-permute-start.10
  52.6 3.1 %collective-permute-start.11 = (f32[150,256]{1,0:T(8,128)S(1)}, f32[150,256]{1,0:T(8,128)S(1)}, u32[]{:S(2)}, u32[]{:S(2)}) collective-permute-start(f32[150,256]{1,0:T(8,128)S(1)} %get-tuple-element.73), channel_id=1, source_target_pairs={{1,2},{2,1},{3,4},{4,3},{5,6},{6,5},{7,8},{8,7},{9,10},{10,9},{11,... | collective-permute-start | bytes 460808 | tf_op jit(solution)/shard_map/ppermute | solution.py:502
  55.7 0.1 shard_map.72
  55.9 1.6 %collective-permute-start.8 = (f32[150,256]{1,0:T(8,128)S(1)}, f32[150,256]{1,0:T(8,128)S(1)}, u32[]{:S(2)}, u32[]{:S(2)}) collective-permute-start(f32[150,256]{1,0:T(8,128)S(1)} %get-tuple-element.70), channel_id=1, source_target_pairs={{0,16},{16,0},{32,48},{48,32},{64,80},{80,64},{96,112},{112,96},{1... | collective-permute-start | bytes 460808 | tf_op jit(solution)/shard_map/ppermute | solution.py:502
  57.4 0.0 collective-permute-start.9
  57.4 1.2 %shard_map.71 = (f32[125,6,256]{2,1,0:T(8,128)S(1)}, f32[125,6,256]{2,1,0:T(8,128)S(1)}) custom-call(f32[125,6,256]{2,1,0:T(8,128)S(1)} %get-tuple-element.67.v, f32[125,6,256]{2,1,0:T(8,128)S(1)} %get-tuple-element.58.c0, f32[125,6,256]{2,1,0:T(8,128)S(1)} %get-tuple-element.59.c1, ...), custom_call_target="tpu_custom_call", output_to_operand_aliasing={{0}: (4, {})} | custom-call | flops 10000000 | bytes 5376000 | tf_op jit(solution)/shard_map/pallas_call | solution.py:481
  58.6 0.0 collective-permute-done.10.ya
  58.7 1.5 %collective-permute-done.11.yb = f32[150,256]{1,0:T(8,128)S(1)} collective-permute-done((f32[150,256]{1,0:T(8,128)S(1)}, f32[150,256]{1,0:T(8,128)S(1)}, u32[]{:S(2)}, u32[]{:S(2)}) %collective-permute-start.11) | collective-permute-done | bytes 153632 | tf_op jit(solution)/shard_map/ppermute | solution.py:502
  60.1 0.0 collective-permute-done.8.xa
  60.1 2.3 %collective-permute-done.9.xb = f32[150,256]{1,0:T(8,128)S(1)} collective-permute-done((f32[150,256]{1,0:T(8,128)S(1)}, f32[150,256]{1,0:T(8,128)S(1)}, u32[]{:S(2)}, u32[]{:S(2)}) %collective-permute-start.9) | collective-permute-done | bytes 153632 | tf_op jit(solution)/shard_map/ppermute | solution.py:502
  62.4 0.3 shard_map.73
  62.7 0.1 shard_map.75
  62.8 0.1 collective-permute-start.14
  62.9 2.4 %collective-permute-start.15 = (f32[150,256]{1,0:T(8,128)S(1)}, f32[150,256]{1,0:T(8,128)S(1)}, u32[]{:S(2)}, u32[]{:S(2)}) collective-permute-start(f32[150,256]{1,0:T(8,128)S(1)} %get-tuple-element.81), channel_id=1, source_target_pairs={{1,2},{2,1},{3,4},{4,3},{5,6},{6,5},{7,8},{8,7},{9,10},{10,9},{11,... | collective-permute-start | bytes 460808 | tf_op jit(solution)/shard_map/ppermute | solution.py:502
  65.3 1.3 %collective-permute-start.12 = (f32[150,256]{1,0:T(8,128)S(1)}, f32[150,256]{1,0:T(8,128)S(1)}, u32[]{:S(2)}, u32[]{:S(2)}) collective-permute-start(f32[150,256]{1,0:T(8,128)S(1)} %get-tuple-element.78), channel_id=1, source_target_pairs={{0,16},{16,0},{32,48},{48,32},{64,80},{80,64},{96,112},{112,96},{1... | collective-permute-start | bytes 460808 | tf_op jit(solution)/shard_map/ppermute | solution.py:502
  66.6 0.0 collective-permute-start.13
  66.6 1.2 %shard_map.74 = (f32[125,6,256]{2,1,0:T(8,128)S(1)}, f32[125,6,256]{2,1,0:T(8,128)S(1)}) custom-call(f32[125,6,256]{2,1,0:T(8,128)S(1)} %get-tuple-element.74.v, f32[125,6,256]{2,1,0:T(8,128)S(1)} %get-tuple-element.58.c0, f32[125,6,256]{2,1,0:T(8,128)S(1)} %get-tuple-element.59.c1, ...), custom_call_target="tpu_custom_call", output_to_operand_aliasing={{0}: (4, {})} | custom-call | flops 10000000 | bytes 5376000 | tf_op jit(solution)/shard_map/pallas_call | solution.py:481
  67.8 0.0 collective-permute-done.14.ya
  67.8 3.0 %collective-permute-done.15.yb = f32[150,256]{1,0:T(8,128)S(1)} collective-permute-done((f32[150,256]{1,0:T(8,128)S(1)}, f32[150,256]{1,0:T(8,128)S(1)}, u32[]{:S(2)}, u32[]{:S(2)}) %collective-permute-start.15) | collective-permute-done | bytes 153632 | tf_op jit(solution)/shard_map/ppermute | solution.py:502
  70.8 0.0 collective-permute-done.12.xa
  70.8 0.7 collective-permute-done.13.xb
  71.6 1.3 %shard_map.76 = (f32[125,6,256]{2,1,0:T(8,128)S(1)}, f32[6,125,1,256]{3,2,1,0:T(1,128)}) custom-call(f32[125,6,256]{2,1,0:T(8,128)S(1)} %get-tuple-element.76.w_in, f32[125,6,256]{2,1,0:T(8,128)S(1)} %get-tuple-element.77.acc, f32[150,256]{1,0:T(8,128)S(1)} %collective-permute-done.12.xa, ...), custom_call_target="tpu_custom_call", output_to_operand_aliasing={{0}: (0, {})} | custom-call | bytes 3686400 | tf_op jit(solution)/shard_map/pallas_call | solution.py:481
Async XLA Ops:
  0.0 1.1 %copy-start = (f32[3,2,5,5,5,1,1,256]{7,6,5,4,3,2,1,0:T(1,128)S(1)}, f32[3,2,5,5,5,1,1,256]{7,6,5,4,3,2,1,0:T(1,128)}, u32[]{:S(2)}) copy-start(f32[3,2,5,5,5,1,1,256]{7,6,5,4,3,2,1,0:T(1,128)} %param.7) | copy-start | bytes 2304004
  1.1 1.1 %copy-start.1 = (f32[3,2,5,5,5,1,1,256]{7,6,5,4,3,2,1,0:T(1,128)S(1)}, f32[3,2,5,5,5,1,1,256]{7,6,5,4,3,2,1,0:T(1,128)}, u32[]{:S(2)}) copy-start(f32[3,2,5,5,5,1,1,256]{7,6,5,4,3,2,1,0:T(1,128)} %param.6) | copy-start | bytes 2304004
  3.9 7.5 %collective-permute-start = (f32[250,256]{1,0:T(8,128)S(1)}, f32[250,256]{1,0:T(8,128)S(1)}, u32[]{:S(2)}, u32[]{:S(2)}) collective-permute-start(f32[250,256]{1,0:T(8,128)S(1)} %get-tuple-element.49), channel_id=1, source_target_pairs={{0,16},{16,0},{32,48},{48,32},{64,80},{80,64},{96,112},{112,96},{1... | collective-permute-start | bytes 768008 | tf_op jit(solution)/shard_map/ppermute | solution.py:502
  7.2 6.1 %collective-permute-start.1 = (f32[250,256]{1,0:T(8,128)S(1)}, f32[250,256]{1,0:T(8,128)S(1)}, u32[]{:S(2)}, u32[]{:S(2)}) collective-permute-start(f32[250,256]{1,0:T(8,128)S(1)} %get-tuple-element.50), channel_id=1, source_target_pairs={{16,32},{32,16},{48,64},{64,48},{80,96},{96,80},{112,128},{128,112... | collective-permute-start | bytes 768008 | tf_op jit(solution)/shard_map/ppermute | solution.py:502
  7.2 0.7 copy-start.2
  7.2 0.7 copy-start.3
  7.2 0.7 copy-start.4
  7.2 0.7 copy-start.5
  13.5 28.7 %collective-permute-start.2 = (f32[270,256]{1,0:T(8,128)S(1)}, f32[270,256]{1,0:T(8,128)S(1)}, u32[]{:S(2)}, u32[]{:S(2)}) collective-permute-start(f32[270,256]{1,0:T(8,128)S(1)} %get-tuple-element.54), channel_id=1, source_target_pairs={{0,1},{1,0},{2,3},{3,2},{4,5},{5,4},{6,7},{7,6},{8,9},{9,8},{10,11... | collective-permute-start | bytes 829448 | tf_op jit(solution)/shard_map/ppermute | solution.py:502
  13.6 28.6 %collective-permute-start.3 = (f32[270,256]{1,0:T(8,128)S(1)}, f32[270,256]{1,0:T(8,128)S(1)}, u32[]{:S(2)}, u32[]{:S(2)}) collective-permute-start(f32[270,256]{1,0:T(8,128)S(1)} %get-tuple-element.55), channel_id=1, source_target_pairs={{1,2},{2,1},{3,4},{4,3},{5,6},{6,5},{7,8},{8,7},{9,10},{10,9},{11,... | collective-permute-start | bytes 829448 | tf_op jit(solution)/shard_map/ppermute | solution.py:502
  43.7 5.3 %collective-permute-start.6 = (f32[150,256]{1,0:T(8,128)S(1)}, f32[150,256]{1,0:T(8,128)S(1)}, u32[]{:S(2)}, u32[]{:S(2)}) collective-permute-start(f32[150,256]{1,0:T(8,128)S(1)} %get-tuple-element.65), channel_id=1, source_target_pairs={{0,1},{1,0},{2,3},{3,2},{4,5},{5,4},{6,7},{7,6},{8,9},{9,8},{10,11... | collective-permute-start | bytes 460808 | tf_op jit(solution)/shard_map/ppermute | solution.py:502
  44.1 8.1 %collective-permute-start.7 = (f32[150,256]{1,0:T(8,128)S(1)}, f32[150,256]{1,0:T(8,128)S(1)}, u32[]{:S(2)}, u32[]{:S(2)}) collective-permute-start(f32[150,256]{1,0:T(8,128)S(1)} %get-tuple-element.66), channel_id=1, source_target_pairs={{1,2},{2,1},{3,4},{4,3},{5,6},{6,5},{7,8},{8,7},{9,10},{10,9},{11,... | collective-permute-start | bytes 460808 | tf_op jit(solution)/shard_map/ppermute | solution.py:502
  45.1 7.1 %collective-permute-start.4 = (f32[150,256]{1,0:T(8,128)S(1)}, f32[150,256]{1,0:T(8,128)S(1)}, u32[]{:S(2)}, u32[]{:S(2)}) collective-permute-start(f32[150,256]{1,0:T(8,128)S(1)} %get-tuple-element.63), channel_id=1, source_target_pairs={{0,16},{16,0},{32,48},{48,32},{64,80},{80,64},{96,112},{112,96},{1... | collective-permute-start | bytes 460808 | tf_op jit(solution)/shard_map/ppermute | solution.py:502
  46.9 5.3 %collective-permute-start.5 = (f32[150,256]{1,0:T(8,128)S(1)}, f32[150,256]{1,0:T(8,128)S(1)}, u32[]{:S(2)}, u32[]{:S(2)}) collective-permute-start(f32[150,256]{1,0:T(8,128)S(1)} %get-tuple-element.64), channel_id=1, source_target_pairs={{16,32},{32,16},{48,64},{64,48},{80,96},{96,80},{112,128},{128,112... | collective-permute-start | bytes 460808 | tf_op jit(solution)/shard_map/ppermute | solution.py:502
  52.5 6.1 %collective-permute-start.10 = (f32[150,256]{1,0:T(8,128)S(1)}, f32[150,256]{1,0:T(8,128)S(1)}, u32[]{:S(2)}, u32[]{:S(2)}) collective-permute-start(f32[150,256]{1,0:T(8,128)S(1)} %get-tuple-element.72), channel_id=1, source_target_pairs={{0,1},{1,0},{2,3},{3,2},{4,5},{5,4},{6,7},{7,6},{8,9},{9,8},{10,11... | collective-permute-start | bytes 460808 | tf_op jit(solution)/shard_map/ppermute | solution.py:502
  52.6 7.5 %collective-permute-start.11 = (f32[150,256]{1,0:T(8,128)S(1)}, f32[150,256]{1,0:T(8,128)S(1)}, u32[]{:S(2)}, u32[]{:S(2)}) collective-permute-start(f32[150,256]{1,0:T(8,128)S(1)} %get-tuple-element.73), channel_id=1, source_target_pairs={{1,2},{2,1},{3,4},{4,3},{5,6},{6,5},{7,8},{8,7},{9,10},{10,9},{11,... | collective-permute-start | bytes 460808 | tf_op jit(solution)/shard_map/ppermute | solution.py:502
  55.9 4.3 %collective-permute-start.8 = (f32[150,256]{1,0:T(8,128)S(1)}, f32[150,256]{1,0:T(8,128)S(1)}, u32[]{:S(2)}, u32[]{:S(2)}) collective-permute-start(f32[150,256]{1,0:T(8,128)S(1)} %get-tuple-element.70), channel_id=1, source_target_pairs={{0,16},{16,0},{32,48},{48,32},{64,80},{80,64},{96,112},{112,96},{1... | collective-permute-start | bytes 460808 | tf_op jit(solution)/shard_map/ppermute | solution.py:502
  57.4 5.0 %collective-permute-start.9 = (f32[150,256]{1,0:T(8,128)S(1)}, f32[150,256]{1,0:T(8,128)S(1)}, u32[]{:S(2)}, u32[]{:S(2)}) collective-permute-start(f32[150,256]{1,0:T(8,128)S(1)} %get-tuple-element.71), channel_id=1, source_target_pairs={{16,32},{32,16},{48,64},{64,48},{80,96},{96,80},{112,128},{128,112... | collective-permute-start | bytes 460808 | tf_op jit(solution)/shard_map/ppermute | solution.py:502
  62.8 5.0 %collective-permute-start.14 = (f32[150,256]{1,0:T(8,128)S(1)}, f32[150,256]{1,0:T(8,128)S(1)}, u32[]{:S(2)}, u32[]{:S(2)}) collective-permute-start(f32[150,256]{1,0:T(8,128)S(1)} %get-tuple-element.80), channel_id=1, source_target_pairs={{0,1},{1,0},{2,3},{3,2},{4,5},{5,4},{6,7},{7,6},{8,9},{9,8},{10,11... | collective-permute-start | bytes 460808 | tf_op jit(solution)/shard_map/ppermute | solution.py:502
  62.9 7.9 %collective-permute-start.15 = (f32[150,256]{1,0:T(8,128)S(1)}, f32[150,256]{1,0:T(8,128)S(1)}, u32[]{:S(2)}, u32[]{:S(2)}) collective-permute-start(f32[150,256]{1,0:T(8,128)S(1)} %get-tuple-element.81), channel_id=1, source_target_pairs={{1,2},{2,1},{3,4},{4,3},{5,6},{6,5},{7,8},{8,7},{9,10},{10,9},{11,... | collective-permute-start | bytes 460808 | tf_op jit(solution)/shard_map/ppermute | solution.py:502
  65.3 5.5 %collective-permute-start.12 = (f32[150,256]{1,0:T(8,128)S(1)}, f32[150,256]{1,0:T(8,128)S(1)}, u32[]{:S(2)}, u32[]{:S(2)}) collective-permute-start(f32[150,256]{1,0:T(8,128)S(1)} %get-tuple-element.78), channel_id=1, source_target_pairs={{0,16},{16,0},{32,48},{48,32},{64,80},{80,64},{96,112},{112,96},{1... | collective-permute-start | bytes 460808 | tf_op jit(solution)/shard_map/ppermute | solution.py:502
  66.6 5.0 %collective-permute-start.13 = (f32[150,256]{1,0:T(8,128)S(1)}, f32[150,256]{1,0:T(8,128)S(1)}, u32[]{:S(2)}, u32[]{:S(2)}) collective-permute-start(f32[150,256]{1,0:T(8,128)S(1)} %get-tuple-element.79), channel_id=1, source_target_pairs={{16,32},{32,16},{48,64},{64,48},{80,96},{96,80},{112,128},{128,112... | collective-permute-start | bytes 460808 | tf_op jit(solution)/shard_map/ppermute | solution.py:502

commit v2 on v1

--- a/solution.py
+++ b/solution.py
@@ -95,10 +95,14 @@
     return jnp.where(odd_row, two[1:2], two[0:1])
 
 
+def z_pair(line):
+    line[0], line[4] = line[0] + pltpu.roll(line[4], 1, 1), line[4] + pltpu.roll(line[0], EZ - 1, 1)
+
+
 def z_sum(ref, ij):
-    low, high = ref[ij * NP], ref[ij * NP + 4]
-    ref[ij * NP] = low + pltpu.roll(high, 1, 1)
-    ref[ij * NP + 4] = high + pltpu.roll(low, EZ - 1, 1)
+    line = [ref[ij * NP + k] for k in range(NP)]
+    z_pair(line)
+    ref[ij * NP], ref[ij * NP + 4] = line[0], line[4]
 
 
 def face_scale(lane, a, b, n, m):
@@ -133,17 +137,17 @@
     ]
 
 
-def opening_kernel(vel, conv, u8, xa, xb, cbuf, sem):
+def opening_kernel(vel, conv, u8, cbuf, xa, xb, sem):
     a, b, n, m, ea, eb, ia, ja, sx, sy = place()
     copies = row_copies(vel, u8, sem.at[0], 0, PTS)
     faces = row_copies(conv, cbuf, sem.at[1], 0, 25) + row_copies(conv, cbuf, sem.at[2], 100, 25)
-    for c in copies + faces:
+    inner = row_copies(conv, cbuf, sem.at[3], 25, 75)
+    for c in copies + faces + inner:
         c.start()
     lane, odd_row = lane_index(), row_index() % 2 == 1
     scale = face_scale(lane, a, b, n, m)
     for c in copies + faces:
         c.wait()
-    done = {}
     for i in (0, 4):
         gs, gt = {}, {}
         for k in range(NP):
@@ -155,23 +159,30 @@
             for k in range(NP):
                 gt[j, k] = line[k]
         for j in range(NP):
-            for k in range(NP):
-                cc = cbuf[pt(i, j, k), 0:ROWS] * scale(i, j, k)
+            w, cc = [], []
+            for k in range(NP):
+                c = cbuf[pt(i, j, k), 0:ROWS] * scale(i, j, k)
                 ends = end_derivatives([u8[pt(q, j, k), 0:ROWS] for q in range(NP)])
-                w = (
-                    widen(cc[0:2], odd_row) * ends[i // 4]
-                    + widen(cc[2:4], odd_row) * gs[j, k]
-                    + widen(cc[4:6], odd_row) * gt[j, k]
+                w.append(
+                    widen(c[0:2], odd_row) * ends[i // 4]
+                    + widen(c[2:4], odd_row) * gs[j, k]
+                    + widen(c[4:6], odd_row) * gt[j, k]
                 )
+                cc.append(c)
+            z_pair(w)
+            c1 = [c[2:4] for c in cc]
+            z_pair(c1)
+            for k in range(NP):
                 r = (j * NP + k) * 10
                 if i == 0:
-                    xa[r : r + 6], xa[r + 6 : r + 10] = w, cc[2:6]
+                    xa[r : r + 6], xa[r + 6 : r + 8], xa[r + 8 : r + 10] = w[k], c1[k], cc[k][4:6]
                 else:
-                    low, clow = xa[r : r + 6], xa[r + 6 : r + 10]
-                    xa[r : r + 6] = jnp.where(ea, w, low)
-                    xa[r + 6 : r + 10] = jnp.where(ea, cc[2:6], clow)
-                    xb[r : r + 6] = jnp.where(ea, low, w) * sx
-                    xb[r + 6 : r + 10] = jnp.where(ea, clow, cc[2:6]) * sx
+                    for lo, hi, new in ((0, 6, w[k]), (6, 8, c1[k]), (8, 10, cc[k][4:6])):
+                        old = xa[r + lo : r + hi]
+                        xa[r + lo : r + hi] = jnp.where(ea, new, old)
+                        xb[r + lo : r + hi] = jnp.where(ea, old, new) * sx
+    for c in inner:
+        c.wait()
 
 
 def coefficients(u8, cbuf, c0, c1, c2, w):
@@ -199,17 +210,16 @@
     for i in range(NP):
         for j in range(NP):
             g = line_derivative(pinned_line([u8[pt(i, j, k), 0:ROWS] for k in range(NP)], lane))
-            for k in range(NP):
-                w[pt(i, j, k)] += c2[pt(i, j, k)] * g[k]
-
-
-def query_kernel(u8, conv, donor, coords, dest, target, table, c0, c1, c2, w, cbuf, sem):
-    copies = row_copies(conv, cbuf, sem, 0, PTS)
-    for c in copies:
-        c.start()
+            line = [w[pt(i, j, k)] + c2[pt(i, j, k)] * g[k] for k in range(NP)]
+            z_pair(line)
+            for k in range(NP):
+                w[pt(i, j, k)] = line[k]
+            z_sum(c0, i * NP + j)
+            z_sum(c1, i * NP + j)
+
+
+def query_kernel(u8, cbuf, donor, coords, dest, target, table, c0, c1, c2, w):
     make_table(u8, donor, coords, dest, target, table)
-    for c in copies:
-        c.wait()
     coefficients(u8, cbuf, c0, c1, c2, w)
 
 
@@ -310,9 +320,9 @@
     table[...] = jnp.concatenate(slots, axis=0).T
 
 
-def third_kernel(w_in, c0_in, c1_in, c2_in, u8, xa, xb, ya, yb, table, v, c0, c1, c2, acc, oya, oyb, z):
-    a, b, n, m, ea, eb, ia, ja, sx, sy = place()
-    del w_in, c0_in, c1_in, c2_in
+def third_kernel(w_in, c0_in, c1_in, c2, xa, xb, ya, yb, table, v, c0, c1, z, oxa, oxb, oya, oyb, e):
+    a, b, n, m, ea, eb, ia, ja, sx, sy = place()
+    del w_in, c0_in, c1_in
     lane, row = lane_index(), row_index()
     odd_row = row % 2 == 1
     got = table[...].T
@@ -347,46 +357,36 @@
         zz = z[ij]
         for k in range(NP):
             p = ij * NP + k
-            v[p] += c2[p] * (zz * slope[k])
-            u = u8[p, 0:ROWS]
-            if k == 0:
-                u = jnp.where(lane == 0, zz, u)
-            if k == 4:
-                u = jnp.where(lane == EZ - 1, zz, u)
-            acc[p] = u
+            e[p] = c2[p] * (zz * slope[k])
     for src, face, z0 in ((xa, ia, 25), (xb, ib, 30)):
         for j in range(NP):
             zz = z[z0 + j]
             for k in range(NP):
-                r = (j * NP + k) * 10
-                p = face * 25 + j * NP + k
-                extra = widen(src[r + 8 : r + 10], odd_row)
-                v[p] += src[r : r + 6] + extra * (zz * slope[k])
+                r, p = (j * NP + k) * 10, face * 25 + j * NP + k
+                v[p] += src[r : r + 6]
                 c1[p] += widen(src[r + 6 : r + 8], odd_row)
-                c2[p] += extra
+                e[p] += widen(src[r + 8 : r + 10], odd_row) * (zz * slope[k])
     for src, face, z0, zd in ((ya, ja, 35, 45), (yb, jb, 40, 47)):
         for i in range(NP):
             zz = z[z0 + i]
             for k in range(NP):
-                r = (i * NP + k) * 10
-                p = i * 25 + face * NP + k
-                extra = widen(src[r + 8 : r + 10], odd_row)
-                add = src[r : r + 6] + extra * (zz * slope[k])
+                r, p = (i * NP + k) * 10, i * 25 + face * NP + k
+                v[p] += src[r : r + 6]
+                c0[p] += widen(src[r + 6 : r + 8], odd_row)
+                add = widen(src[r + 8 : r + 10], odd_row) * (zz * slope[k])
                 if i in (0, 4):
                     r = 250 + ((i // 4) * NP + k) * 2
-                    far = widen(src[r : r + 2], odd_row)
                     through_a = ea if i == 4 else jnp.logical_not(ea)
                     zfar = jnp.where(through_a, z[zd], z[zd + 1])
-                    add = add + far * (zfar * slope[k])
-                    extra = extra + far
-                v[p] += add
-                c0[p] += widen(src[(i * NP + k) * 10 + 6 : (i * NP + k) * 10 + 8], odd_row)
-                c2[p] += extra
+                    add = add + widen(src[r : r + 2], odd_row) * (zfar * slope[k])
+                e[p] += add
     for ij in range(25):
-        z_sum(v, ij)
-        z_sum(c0, ij)
-        z_sum(c1, ij)
+        line = [e[ij * NP + k] for k in range(NP)]
+        z_pair(line)
+        for k in range(NP):
+            v[ij * NP + k] += line[k]
     second_messages(v, c1, oya, oyb)
+    first_messages(v, c0, oxa, oxb)
 
 
 def second_messages(v, c1, oya, oyb):
@@ -423,22 +423,60 @@
                 v[i * 25 + face * NP + k] += src[r : r + 6]
 
 
-def send_kernel(w_in, c1, xa, xb, ya, yb, v, oya, oyb):
+def send_kernel(w_in, c0, c1, ya, yb, xb, xa, v, oxa, oxb, oya, oyb):
     del w_in
     take_messages(v, xa, xb, ya, yb)
     second_messages(v, c1, oya, oyb)
+    first_messages(v, c0, oxa, oxb)
+
+
+def sum_third(c2, xa, xb, ya, yb):
+    a, b, n, m, ea, eb, ia, ja, sx, sy = place()
+    odd_row = row_index() % 2 == 1
+    for src, face in ((xa, ia), (xb, 4 - ia)):
+        for jk in range(25):
+            c2[face * 25 + jk] += widen(src[jk * 10 + 8 : jk * 10 + 10], odd_row)
+    for src, face in ((ya, ja), (yb, 4 - ja)):
+        for i in range(NP):
+            for k in range(NP):
+                r = (i * NP + k) * 10 + 8
+                extra = src[r : r + 2]
+                if i in (0, 4):
+                    far = 250 + ((i // 4) * NP + k) * 2
+                    extra = extra + src[far : far + 2]
+                c2[i * 25 + face * NP + k] += widen(extra, odd_row)
+
+
+def local_first_kernel(coef, v, c0, c1, c2_in, u8, z, xa, xb, ya, yb, acc, w, c2):
+    del c2_in
+    sum_third(c2, xa, xb, ya, yb)
+    lane = lane_index()
+    for ij in range(25):
+        for k in range(NP):
+            p = ij * NP + k
+            u = u8[p, 0:ROWS]
+            if k == 0:
+                u = jnp.where(lane == 0, z[ij], u)
+            if k == 4:
+                u = jnp.where(lane == EZ - 1, z[ij], u)
+            acc[p] = u + v[p] * coef
+    apply(v, c0, c1, c2, w)
 
 
 def local_kernel(coef, v, c0, c1, c2, acc_in, acc, w):
     del acc_in
+    for p in range(PTS):
+        acc[p] += v[p] * coef
+    apply(v, c0, c1, c2, w)
+
+
+def apply(v, c0, c1, c2, w):
     for j in range(NP):
         for k in range(NP):
             u = [v[pt(i, j, k)] for i in range(NP)]
             g = line_derivative(u)
             for i in range(NP):
-                p = pt(i, j, k)
-                acc[p] += u[i] * coef
-                w[p] = c0[p] * g[i]
+                w[pt(i, j, k)] = c0[pt(i, j, k)] * g[i]
     for i in range(NP):
         for k in range(NP):
             g = line_derivative([v[pt(i, j, k)] for j in range(NP)])
@@ -448,12 +486,12 @@
         for j in range(NP):
             g = line_derivative([v[pt(i, j, k)] for k in range(NP)])
             t = [c2[pt(i, j, k)] * g[k] for k in range(NP)]
-            t[0], t[4] = t[0] + pltpu.roll(t[4], 1, 1), t[4] + pltpu.roll(t[0], EZ - 1, 1)
+            z_pair(t)
             for k in range(NP):
                 w[pt(i, j, k)] += t[k]
 
 
-def last_kernel(coef, w_in, acc, xa, xb, ya, yb, v, out, obuf, sem):
+def last_kernel(coef, w_in, acc, ya, yb, xb, xa, v, out, obuf, sem):
     del w_in
     take_messages(v, xa, xb, ya, yb)
     started = []
@@ -475,7 +513,7 @@
 RAW = (ROWS, PTS, 1, EZ)
 
 
-def call(kernel, outs, args, aliases=None, scratch=(), flops=0):
+def call(kernel, outs, args, aliases=None, scratch=(), flops=0, limit=24):
     moved = sum(4 * math.prod(x.shape) for x in args) + sum(4 * math.prod(s) for s in outs)
     spec = lambda shape: pl.BlockSpec(memory_space=pl.ANY if shape == RAW else pltpu.VMEM)
     return pl.pallas_call(
@@ -485,7 +523,7 @@
         out_specs=[spec(s) for s in outs],
         input_output_aliases=aliases or {},
         scratch_shapes=list(scratch),
-        compiler_params=pltpu.CompilerParams(vmem_limit_bytes=24 * 1024 * 1024),
+        compiler_params=pltpu.CompilerParams(vmem_limit_bytes=limit * 1024 * 1024),
         cost_estimate=pl.CostEstimate(flops=flops, bytes_accessed=moved, transcendentals=0),
     )(*args)
 
@@ -510,54 +548,64 @@
     devices = lax.axis_size("gx") * lax.axis_size("gy")
     queries = dest_rank.shape[0]
     vel, conv = velocity.reshape(RAW), convecting.reshape(RAW)
+    vel, conv = (pltpu.with_memory_space_constraint(x, pltpu.HBM) for x in (vel, conv))
     whole = pltpu.VMEM((PTS, 8, EZ), f32)
-    u8, xa, xb = call(
+    u8, cbuf, xa, xb = call(
         opening_kernel,
-        [(PTS, 8, EZ)] + [(250, EZ)] * 2,
+        [(PTS, 8, EZ)] * 2 + [(250, EZ)] * 2,
         [vel, conv],
-        scratch=[whole, pltpu.SemaphoreType.DMA((3, ROWS))],
+        scratch=[pltpu.SemaphoreType.DMA((4, ROWS))],
+        limit=24,
     )
-    xa, xb = swap(xa, "gx", 0), swap(xb, "gx", 1)
+    fxa, fxb = swap(xa, "gx", 0), swap(xb, "gx", 1)
     table, c0, c1, c2, w = call(
         query_kernel,
         [(devices, 128)] + [FIELD] * 4,
         [
             u8,
-            conv,
+            cbuf,
             donor_element.reshape(1, queries),
             coords,
             dest_rank.reshape(1, queries),
             target.reshape(1, queries),
         ],
-        scratch=[whole, pltpu.SemaphoreType.DMA((ROWS,))],
     )
-    ya, yb = call(second_kernel, [(270, EZ)] * 2, [w, c0, c2, xa, xb])
+    ya, yb = call(second_kernel, [(270, EZ)] * 2, [w, c0, c2, fxa, fxb])
     table, ya, yb = lax.optimization_barrier((table, ya, yb))
-    ya, yb = swap(ya, "gy", 0), swap(yb, "gy", 1)
+    fya, fyb = swap(ya, "gy", 0), swap(yb, "gy", 1)
     table = lax.all_to_all(table.reshape(devices, 1, 128), ("gx", "gy"), 0, 0).reshape(devices, 128)
-    v, c0, c1, c2, acc, ya, yb = call(
+    v, c0, c1, z, xa, xb, ya, yb = call(
         third_kernel,
-        [FIELD] * 5 + [(150, EZ)] * 2,
-        [w, c0, c1, c2, u8, xa, xb, ya, yb, table],
-        aliases={0: 0, 1: 1, 2: 2, 3: 3},
-        scratch=[pltpu.VMEM((49, ROWS, EZ), f32)],
+        [FIELD] * 3 + [(49, ROWS, EZ)] + [(150, EZ)] * 4,
+        [w, c0, c1, c2, fxa, fxb, fya, fyb, table],
+        aliases={0: 0, 1: 1, 2: 2},
+        scratch=[pltpu.VMEM(FIELD, f32)],
     )
     coef = 1.0
     for stage in range(1, 4):
         coef = coef * time_step / stage
+        xa, xb = swap(xa, "gx", 0), swap(xb, "gx", 1)
         ya, yb = swap(ya, "gy", 0), swap(yb, "gy", 1)
-        xa, xb = call(first_messages, [(150, EZ)] * 2, [v, c0])
-        got = [swap(xa, "gx", 0), swap(xb, "gx", 1), ya, yb]
-        acc, w = call(
-            functools.partial(local_kernel, coef),
-            [FIELD] * 2,
-            [v, c0, c1, c2, acc],
-            aliases={4: 0},
-            flops=10**7,
-        )
+        got = [ya, yb, xb, xa]
+        if stage == 1:
+            acc, w, c2 = call(
+                functools.partial(local_first_kernel, coef),
+                [FIELD] * 3,
+                [v, c0, c1, c2, u8, z, fxa, fxb, fya, fyb],
+                aliases={3: 2},
+                flops=10**7,
+            )
+        else:
+            acc, w = call(
+                functools.partial(local_kernel, coef),
+                [FIELD] * 2,
+                [v, c0, c1, c2, acc],
+                aliases={4: 0},
+                flops=10**7,
+            )
         if stage < 3:
-            v, ya, yb = call(
-                send_kernel, [FIELD] + [(150, EZ)] * 2, [w, c1, *got], aliases={0: 0}
+            v, xa, xb, ya, yb = call(
+                send_kernel, [FIELD] + [(150, EZ)] * 4, [w, c0, c1, *got], aliases={0: 0}
             )
     coef = coef * time_step / 4
     _, out = call(

time: 73.2 us -> 70 us (0.956); the launches traced: 73 us -> 68.7 us
  waiting for transfers between devices: 12.5 us -> 9.01 us
  local copies, waits for them, and re-layouts: 2.94 us -> 0.69 us
  starting transfers between devices: 19.2 us -> 20.1 us
    ppermute x16, waiting for transfers between devices: 12.5 us -> 9.01 us  [swap(): return lax.ppermute(x, axis, pairs(lax.axis_size(axis), offset))]
    unnamed x12 -> x8, local copies, waits for them, and re-layouts: 2.94 us -> 0.69 us
    ppermute x16, starting transfers between devices: 19.2 us -> 20.1 us  [swap(): return lax.ppermute(x, axis, pairs(lax.axis_size(axis), offset))]
    pallas_call x13 -> x10, Pallas kernels: 12.9 us -> 13.4 us  [call(): pl.pallas_call(kernel, out_shape=[jax.ShapeDtypeStruct(s, f32) for s in o...]
where the time goes in v2:
time: 70 us; the launch traced here: 68.7 us
  blocking collectives  25.2 us (36%)
  starting transfers between devices  20.1 us (29%)
  Pallas kernels  13.4 us (19%)
  waiting for transfers between devices  9.01 us (13%)
    all_to_all x1, blocking collectives, body(): lax.all_to_all(table.reshape(devices, 1, 128), ('gx', 'gy'), 0, 0)  25.2 us
    ppermute x16, starting transfers between devices, swap(): return lax.ppermute(x, axis, pairs(lax.axis_size(axis), offset))  20.1 us
    pallas_call x10, Pallas kernels, call(): pl.pallas_call(kernel, out_shape=[jax.ShapeDtypeStruct(s, f32) for s in o...  13.4 us
    ppermute x16, waiting for transfers between devices, swap(): return lax.ppermute(x, axis, pairs(lax.axis_size(axis), offset))  9.01 us
  transfers between devices with their start and end apart: 16, of which 6 were waited for; matrix products, arithmetic and copies ran while one was open for 0% of the time, Pallas kernels for 10%

profile of v2, /device:TPU:1, one launch (start us, length us, event | category | flops | bytes accessed | tf_op | source)
XLA Modules:
  0.0 68.7 jit_solution(10973271538870467694)
XLA Ops:
  0.0 2.2 %shard_map.64 = (f32[125,8,256]{2,1,0:T(8,128)S(1)}, f32[125,8,256]{2,1,0:T(8,128)S(1)}, f32[250,256]{1,0:T(8,128)S(1)}, f32[250,256]{1,0:T(8,128)S(1)}) custom-call(f32[6,125,1,256]{3,2,1,0:T(1,128)} %bitcast.17, f32[6,125,1,256]{3,2,1,0:T(1,128)} %bitcast.18), custom_call_target="tpu_custom_call" | custom-call | bytes 4096000 | tf_op jit(solution)/shard_map/pallas_call | solution.py:519
  2.2 3.3 %collective-permute-start = (f32[250,256]{1,0:T(8,128)S(1)}, f32[250,256]{1,0:T(8,128)S(1)}, u32[]{:S(2)}, u32[]{:S(2)}) collective-permute-start(f32[250,256]{1,0:T(8,128)S(1)} %get-tuple-element.51), channel_id=1, source_target_pairs={{0,16},{16,0},{32,48},{48,32},{64,80},{80,64},{96,112},{112,96},{1... | collective-permute-start | bytes 768008 | tf_op jit(solution)/shard_map/ppermute | solution.py:540
  5.6 0.0 collective-permute-start.1
  5.6 0.0 copy-start
  5.6 0.0 copy-start.1
  5.6 0.0 copy-start.2
  5.6 0.0 copy-start.3
  5.6 0.7 copy-done
  6.2 0.0 copy-done.1
  6.2 0.0 copy-done.2
  6.2 0.0 copy-done.3
  6.3 3.0 %shard_map.65 = (f32[256,128]{1,0:T(8,128)S(1)}, f32[125,6,256]{2,1,0:T(8,128)S(1)}, f32[125,6,256]{2,1,0:T(8,128)S(1)}, f32[125,6,256]{2,1,0:T(8,128)S(1)}, f32[125,6,256]{2,1,0:T(8,128)S(1)}) custom-call(f32[125,8,256]{2,1,0:T(8,128)S(1)} %get-tuple-element.45.u8, f32[125,8,256]{2,1,0:T(8,128)S(1)} %get-tuple-element.46.cbuf, s32[1,100]{1,0:T(1,128)S(1)} %bitcast.14, ...), custom_call_target="tpu_custom_call" | custom-call | bytes 5253472 | tf_op jit(solution)/shard_map/pallas_call | solution.py:519
  9.3 0.0 collective-permute-done.xa
  9.3 2.4 %collective-permute-done.1.xb = f32[250,256]{1,0:T(8,128)S(1)} collective-permute-done((f32[250,256]{1,0:T(8,128)S(1)}, f32[250,256]{1,0:T(8,128)S(1)}, u32[]{:S(2)}, u32[]{:S(2)}) %collective-permute-start.1) | collective-permute-done | bytes 256032 | tf_op jit(solution)/shard_map/ppermute | solution.py:540
  11.6 0.2 shard_map.66
  11.9 0.1 collective-permute-start.2
  12.0 3.3 %collective-permute-start.3 = (f32[270,256]{1,0:T(8,128)S(1)}, f32[270,256]{1,0:T(8,128)S(1)}, u32[]{:S(2)}, u32[]{:S(2)}) collective-permute-start(f32[270,256]{1,0:T(8,128)S(1)} %get-tuple-element.57), channel_id=1, source_target_pairs={{1,2},{2,1},{3,4},{4,3},{5,6},{6,5},{7,8},{8,7},{9,10},{10,9},{11,... | collective-permute-start | bytes 829448 | tf_op jit(solution)/shard_map/ppermute | solution.py:540
  15.3 25.2 %all_to_all.5 = f32[256,1,128]{2,1,0:T(1,128)S(1)} all-to-all(f32[256,1,128]{2,1,0:T(1,128)S(1)} %bitcast.13), channel_id=1, replica_groups=mesh['gx'=16,'gy'=16] {'gx','gy'}, dimensions={0} | all-to-all | bytes 262144 | tf_op jit(solution)/shard_map/all_to_all | solution.py:576
  40.5 0.0 collective-permute-done.2.ya
  40.5 0.0 collective-permute-done.3.yb
  40.5 1.6 %shard_map.67 = (f32[125,6,256]{2,1,0:T(8,128)S(1)}, f32[125,6,256]{2,1,0:T(8,128)S(1)}, f32[125,6,256]{2,1,0:T(8,128)S(1)}, f32[49,6,256]{2,1,0:T(8,128)S(1)}, ...) custom-call(f32[125,6,256]{2,1,0:T(8,128)S(1)} %get-tuple-element.47, ...), custom_call_target="tpu_custom_call", output_to_operand_aliasing={{0}: (0, {}), {1}: (1, {}), {2}: (2, {})} | custom-call | bytes 7487488 | tf_op jit(solution)/shard_map/pallas_call | solution.py:519
  42.1 0.4 collective-permute-start.4
  42.5 0.8 %collective-permute-start.5 = (f32[150,256]{1,0:T(8,128)S(1)}, f32[150,256]{1,0:T(8,128)S(1)}, u32[]{:S(2)}, u32[]{:S(2)}) collective-permute-start(f32[150,256]{1,0:T(8,128)S(1)} %get-tuple-element.65), channel_id=1, source_target_pairs={{1,2},{2,1},{3,4},{4,3},{5,6},{6,5},{7,8},{8,7},{9,10},{10,9},{11,... | collective-permute-start | bytes 460808 | tf_op jit(solution)/shard_map/ppermute | solution.py:540
  43.3 2.3 %collective-permute-start.6 = (f32[150,256]{1,0:T(8,128)S(1)}, f32[150,256]{1,0:T(8,128)S(1)}, u32[]{:S(2)}, u32[]{:S(2)}) collective-permute-start(f32[150,256]{1,0:T(8,128)S(1)} %get-tuple-element.66), channel_id=1, source_target_pairs={{16,32},{32,16},{48,64},{64,48},{80,96},{96,80},{112,128},{128,112... | collective-permute-start | bytes 460808 | tf_op jit(solution)/shard_map/ppermute | solution.py:540
  45.6 0.0 collective-permute-start.7
  45.6 1.6 %shard_map.68 = (f32[125,6,256]{2,1,0:T(8,128)S(1)}, f32[125,6,256]{2,1,0:T(8,128)S(1)}, f32[125,6,256]{2,1,0:T(8,128)S(1)}) custom-call(f32[125,6,256]{2,1,0:T(8,128)S(1)} %get-tuple-element.59.v, f32[125,6,256]{2,1,0:T(8,128)S(1)} %get-tuple-element.60.c0, f32[125,6,256]{2,1,0:T(8,128)S(1)} %get-tuple-element.61.c1, ...), custom_call_target="tpu_custom_call", output_to_operand_aliasing={{2}: (3, {})} | custom-call | flops 10000000 | bytes 7766016 | tf_op jit(solution)/shard_map/pallas_call | solution.py:519
  47.2 0.1 collective-permute-done.4.ya
  47.3 3.3 %collective-permute-done.5.yb = f32[150,256]{1,0:T(8,128)S(1)} collective-permute-done((f32[150,256]{1,0:T(8,128)S(1)}, f32[150,256]{1,0:T(8,128)S(1)}, u32[]{:S(2)}, u32[]{:S(2)}) %collective-permute-start.5) | collective-permute-done | bytes 153632 | tf_op jit(solution)/shard_map/ppermute | solution.py:540
  50.6 0.0 collective-permute-done.6.xb
  50.6 0.0 collective-permute-done.7.xa
  50.6 0.5 shard_map.69
  51.1 0.1 collective-permute-start.8
  51.2 1.8 %collective-permute-start.9 = (f32[150,256]{1,0:T(8,128)S(1)}, f32[150,256]{1,0:T(8,128)S(1)}, u32[]{:S(2)}, u32[]{:S(2)}) collective-permute-start(f32[150,256]{1,0:T(8,128)S(1)} %get-tuple-element.73), channel_id=1, source_target_pairs={{1,2},{2,1},{3,4},{4,3},{5,6},{6,5},{7,8},{8,7},{9,10},{10,9},{11,... | collective-permute-start | bytes 460808 | tf_op jit(solution)/shard_map/ppermute | solution.py:540
  52.9 1.9 %collective-permute-start.10 = (f32[150,256]{1,0:T(8,128)S(1)}, f32[150,256]{1,0:T(8,128)S(1)}, u32[]{:S(2)}, u32[]{:S(2)}) collective-permute-start(f32[150,256]{1,0:T(8,128)S(1)} %get-tuple-element.74), channel_id=1, source_target_pairs={{16,32},{32,16},{48,64},{64,48},{80,96},{96,80},{112,128},{128,112... | collective-permute-start | bytes 460808 | tf_op jit(solution)/shard_map/ppermute | solution.py:540
  54.8 0.4 collective-permute-start.11
  55.2 1.3 %shard_map.70 = (f32[125,6,256]{2,1,0:T(8,128)S(1)}, f32[125,6,256]{2,1,0:T(8,128)S(1)}) custom-call(f32[125,6,256]{2,1,0:T(8,128)S(1)} %get-tuple-element.68.v, f32[125,6,256]{2,1,0:T(8,128)S(1)} %get-tuple-element.60.c0, f32[125,6,256]{2,1,0:T(8,128)S(1)} %get-tuple-element.61.c1, ...), custom_call_target="tpu_custom_call", output_to_operand_aliasing={{0}: (4, {})} | custom-call | flops 10000000 | bytes 5376000 | tf_op jit(solution)/shard_map/pallas_call | solution.py:519
  56.5 0.0 collective-permute-done.8.ya
  56.5 2.1 %collective-permute-done.9.yb = f32[150,256]{1,0:T(8,128)S(1)} collective-permute-done((f32[150,256]{1,0:T(8,128)S(1)}, f32[150,256]{1,0:T(8,128)S(1)}, u32[]{:S(2)}, u32[]{:S(2)}) %collective-permute-start.9) | collective-permute-done | bytes 153632 | tf_op jit(solution)/shard_map/ppermute | solution.py:540
  58.6 0.0 collective-permute-done.10.xb
  58.7 0.0 collective-permute-done.11.xa
  58.7 0.4 shard_map.71
  59.1 0.1 collective-permute-start.12
  59.2 3.4 %collective-permute-start.13 = (f32[150,256]{1,0:T(8,128)S(1)}, f32[150,256]{1,0:T(8,128)S(1)}, u32[]{:S(2)}, u32[]{:S(2)}) collective-permute-start(f32[150,256]{1,0:T(8,128)S(1)} %get-tuple-element.81), channel_id=1, source_target_pairs={{1,2},{2,1},{3,4},{4,3},{5,6},{6,5},{7,8},{8,7},{9,10},{10,9},{11,... | collective-permute-start | bytes 460808 | tf_op jit(solution)/shard_map/ppermute | solution.py:540
  62.6 1.7 %collective-permute-start.14 = (f32[150,256]{1,0:T(8,128)S(1)}, f32[150,256]{1,0:T(8,128)S(1)}, u32[]{:S(2)}, u32[]{:S(2)}) collective-permute-start(f32[150,256]{1,0:T(8,128)S(1)} %get-tuple-element.82), channel_id=1, source_target_pairs={{16,32},{32,16},{48,64},{64,48},{80,96},{96,80},{112,128},{128,112... | collective-permute-start | bytes 460808 | tf_op jit(solution)/shard_map/ppermute | solution.py:540
  64.3 0.5 collective-permute-start.15
  64.8 1.3 %shard_map.72 = (f32[125,6,256]{2,1,0:T(8,128)S(1)}, f32[125,6,256]{2,1,0:T(8,128)S(1)}) custom-call(f32[125,6,256]{2,1,0:T(8,128)S(1)} %get-tuple-element.76.v, f32[125,6,256]{2,1,0:T(8,128)S(1)} %get-tuple-element.60.c0, f32[125,6,256]{2,1,0:T(8,128)S(1)} %get-tuple-element.61.c1, ...), custom_call_target="tpu_custom_call", output_to_operand_aliasing={{0}: (4, {})} | custom-call | flops 10000000 | bytes 5376000 | tf_op jit(solution)/shard_map/pallas_call | solution.py:519
  66.1 0.0 collective-permute-done.12.ya
  66.1 0.6 collective-permute-done.13.yb
  66.7 0.5 collective-permute-done.14.xb
  67.2 0.0 collective-permute-done.15.xa
  67.2 1.3 %shard_map.73 = (f32[125,6,256]{2,1,0:T(8,128)S(1)}, f32[6,125,1,256]{3,2,1,0:T(1,128)}) custom-call(f32[125,6,256]{2,1,0:T(8,128)S(1)} %get-tuple-element.78.w_in, f32[125,6,256]{2,1,0:T(8,128)S(1)} %get-tuple-element.79.acc, f32[150,256]{1,0:T(8,128)S(1)} %collective-permute-done.12.ya, ...), custom_call_target="tpu_custom_call", output_to_operand_aliasing={{0}: (0, {})} | custom-call | bytes 3686400 | tf_op jit(solution)/shard_map/pallas_call | solution.py:519
Async XLA Ops:
  2.2 7.1 %collective-permute-start = (f32[250,256]{1,0:T(8,128)S(1)}, f32[250,256]{1,0:T(8,128)S(1)}, u32[]{:S(2)}, u32[]{:S(2)}) collective-permute-start(f32[250,256]{1,0:T(8,128)S(1)} %get-tuple-element.51), channel_id=1, source_target_pairs={{0,16},{16,0},{32,48},{48,32},{64,80},{80,64},{96,112},{112,96},{1... | collective-permute-start | bytes 768008 | tf_op jit(solution)/shard_map/ppermute | solution.py:540
  5.6 6.1 %collective-permute-start.1 = (f32[250,256]{1,0:T(8,128)S(1)}, f32[250,256]{1,0:T(8,128)S(1)}, u32[]{:S(2)}, u32[]{:S(2)}) collective-permute-start(f32[250,256]{1,0:T(8,128)S(1)} %get-tuple-element.52), channel_id=1, source_target_pairs={{16,32},{32,16},{48,64},{64,48},{80,96},{96,80},{112,128},{128,112... | collective-permute-start | bytes 768008 | tf_op jit(solution)/shard_map/ppermute | solution.py:540
  5.6 0.7 copy-start
  5.6 0.7 copy-start.1
  5.6 0.7 copy-start.2
  5.6 0.7 %copy-start.3 = (s32[100]{0:T(128)S(1)}, s32[100]{0:T(128)}, u32[]{:S(2)}) copy-start(s32[100]{0:T(128)} %param.11) | copy-start | bytes 1204
  11.9 28.7 %collective-permute-start.2 = (f32[270,256]{1,0:T(8,128)S(1)}, f32[270,256]{1,0:T(8,128)S(1)}, u32[]{:S(2)}, u32[]{:S(2)}) collective-permute-start(f32[270,256]{1,0:T(8,128)S(1)} %get-tuple-element.56), channel_id=1, source_target_pairs={{0,1},{1,0},{2,3},{3,2},{4,5},{5,4},{6,7},{7,6},{8,9},{9,8},{10,11... | collective-permute-start | bytes 829448 | tf_op jit(solution)/shard_map/ppermute | solution.py:540
  12.0 28.6 %collective-permute-start.3 = (f32[270,256]{1,0:T(8,128)S(1)}, f32[270,256]{1,0:T(8,128)S(1)}, u32[]{:S(2)}, u32[]{:S(2)}) collective-permute-start(f32[270,256]{1,0:T(8,128)S(1)} %get-tuple-element.57), channel_id=1, source_target_pairs={{1,2},{2,1},{3,4},{4,3},{5,6},{6,5},{7,8},{8,7},{9,10},{10,9},{11,... | collective-permute-start | bytes 829448 | tf_op jit(solution)/shard_map/ppermute | solution.py:540
  42.1 5.2 %collective-permute-start.4 = (f32[150,256]{1,0:T(8,128)S(1)}, f32[150,256]{1,0:T(8,128)S(1)}, u32[]{:S(2)}, u32[]{:S(2)}) collective-permute-start(f32[150,256]{1,0:T(8,128)S(1)} %get-tuple-element.64), channel_id=1, source_target_pairs={{0,1},{1,0},{2,3},{3,2},{4,5},{5,4},{6,7},{7,6},{8,9},{9,8},{10,11... | collective-permute-start | bytes 460808 | tf_op jit(solution)/shard_map/ppermute | solution.py:540
  42.5 8.1 %collective-permute-start.5 = (f32[150,256]{1,0:T(8,128)S(1)}, f32[150,256]{1,0:T(8,128)S(1)}, u32[]{:S(2)}, u32[]{:S(2)}) collective-permute-start(f32[150,256]{1,0:T(8,128)S(1)} %get-tuple-element.65), channel_id=1, source_target_pairs={{1,2},{2,1},{3,4},{4,3},{5,6},{6,5},{7,8},{8,7},{9,10},{10,9},{11,... | collective-permute-start | bytes 460808 | tf_op jit(solution)/shard_map/ppermute | solution.py:540
  43.3 7.3 %collective-permute-start.6 = (f32[150,256]{1,0:T(8,128)S(1)}, f32[150,256]{1,0:T(8,128)S(1)}, u32[]{:S(2)}, u32[]{:S(2)}) collective-permute-start(f32[150,256]{1,0:T(8,128)S(1)} %get-tuple-element.66), channel_id=1, source_target_pairs={{16,32},{32,16},{48,64},{64,48},{80,96},{96,80},{112,128},{128,112... | collective-permute-start | bytes 460808 | tf_op jit(solution)/shard_map/ppermute | solution.py:540
  45.6 5.0 %collective-permute-start.7 = (f32[150,256]{1,0:T(8,128)S(1)}, f32[150,256]{1,0:T(8,128)S(1)}, u32[]{:S(2)}, u32[]{:S(2)}) collective-permute-start(f32[150,256]{1,0:T(8,128)S(1)} %get-tuple-element.67), channel_id=1, source_target_pairs={{0,16},{16,0},{32,48},{48,32},{64,80},{80,64},{96,112},{112,96},{1... | collective-permute-start | bytes 460808 | tf_op jit(solution)/shard_map/ppermute | solution.py:540
  51.1 5.5 %collective-permute-start.8 = (f32[150,256]{1,0:T(8,128)S(1)}, f32[150,256]{1,0:T(8,128)S(1)}, u32[]{:S(2)}, u32[]{:S(2)}) collective-permute-start(f32[150,256]{1,0:T(8,128)S(1)} %get-tuple-element.72), channel_id=1, source_target_pairs={{0,1},{1,0},{2,3},{3,2},{4,5},{5,4},{6,7},{7,6},{8,9},{9,8},{10,11... | collective-permute-start | bytes 460808 | tf_op jit(solution)/shard_map/ppermute | solution.py:540
  51.2 7.5 %collective-permute-start.9 = (f32[150,256]{1,0:T(8,128)S(1)}, f32[150,256]{1,0:T(8,128)S(1)}, u32[]{:S(2)}, u32[]{:S(2)}) collective-permute-start(f32[150,256]{1,0:T(8,128)S(1)} %get-tuple-element.73), channel_id=1, source_target_pairs={{1,2},{2,1},{3,4},{4,3},{5,6},{6,5},{7,8},{8,7},{9,10},{10,9},{11,... | collective-permute-start | bytes 460808 | tf_op jit(solution)/shard_map/ppermute | solution.py:540
  52.9 5.7 %collective-permute-start.10 = (f32[150,256]{1,0:T(8,128)S(1)}, f32[150,256]{1,0:T(8,128)S(1)}, u32[]{:S(2)}, u32[]{:S(2)}) collective-permute-start(f32[150,256]{1,0:T(8,128)S(1)} %get-tuple-element.74), channel_id=1, source_target_pairs={{16,32},{32,16},{48,64},{64,48},{80,96},{96,80},{112,128},{128,112... | collective-permute-start | bytes 460808 | tf_op jit(solution)/shard_map/ppermute | solution.py:540
  54.8 3.8 %collective-permute-start.11 = (f32[150,256]{1,0:T(8,128)S(1)}, f32[150,256]{1,0:T(8,128)S(1)}, u32[]{:S(2)}, u32[]{:S(2)}) collective-permute-start(f32[150,256]{1,0:T(8,128)S(1)} %get-tuple-element.75), channel_id=1, source_target_pairs={{0,16},{16,0},{32,48},{48,32},{64,80},{80,64},{96,112},{112,96},{1... | collective-permute-start | bytes 460808 | tf_op jit(solution)/shard_map/ppermute | solution.py:540
  59.1 7.0 %collective-permute-start.12 = (f32[150,256]{1,0:T(8,128)S(1)}, f32[150,256]{1,0:T(8,128)S(1)}, u32[]{:S(2)}, u32[]{:S(2)}) collective-permute-start(f32[150,256]{1,0:T(8,128)S(1)} %get-tuple-element.80), channel_id=1, source_target_pairs={{0,1},{1,0},{2,3},{3,2},{4,5},{5,4},{6,7},{7,6},{8,9},{9,8},{10,11... | collective-permute-start | bytes 460808 | tf_op jit(solution)/shard_map/ppermute | solution.py:540
  59.2 7.5 %collective-permute-start.13 = (f32[150,256]{1,0:T(8,128)S(1)}, f32[150,256]{1,0:T(8,128)S(1)}, u32[]{:S(2)}, u32[]{:S(2)}) collective-permute-start(f32[150,256]{1,0:T(8,128)S(1)} %get-tuple-element.81), channel_id=1, source_target_pairs={{1,2},{2,1},{3,4},{4,3},{5,6},{6,5},{7,8},{8,7},{9,10},{10,9},{11,... | collective-permute-start | bytes 460808 | tf_op jit(solution)/shard_map/ppermute | solution.py:540
  62.6 4.7 %collective-permute-start.14 = (f32[150,256]{1,0:T(8,128)S(1)}, f32[150,256]{1,0:T(8,128)S(1)}, u32[]{:S(2)}, u32[]{:S(2)}) collective-permute-start(f32[150,256]{1,0:T(8,128)S(1)} %get-tuple-element.82), channel_id=1, source_target_pairs={{16,32},{32,16},{48,64},{64,48},{80,96},{96,80},{112,128},{128,112... | collective-permute-start | bytes 460808 | tf_op jit(solution)/shard_map/ppermute | solution.py:540
  64.3 2.9 %collective-permute-start.15 = (f32[150,256]{1,0:T(8,128)S(1)}, f32[150,256]{1,0:T(8,128)S(1)}, u32[]{:S(2)}, u32[]{:S(2)}) collective-permute-start(f32[150,256]{1,0:T(8,128)S(1)} %get-tuple-element.83), channel_id=1, source_target_pairs={{0,16},{16,0},{32,48},{48,32},{64,80},{80,64},{96,112},{112,96},{1... | collective-permute-start | bytes 460808 | tf_op jit(solution)/shard_map/ppermute | solution.py:540

commit v3 on v2

--- a/solution.py
+++ b/solution.py
@@ -423,7 +423,7 @@
                 v[i * 25 + face * NP + k] += src[r : r + 6]
 
 
-def send_kernel(w_in, c0, c1, ya, yb, xb, xa, v, oxa, oxb, oya, oyb):
+def send_kernel(w_in, c0, c1, ya, xb, yb, xa, v, oxa, oxb, oya, oyb):
     del w_in
     take_messages(v, xa, xb, ya, yb)
     second_messages(v, c1, oya, oyb)
@@ -491,7 +491,7 @@
                 w[pt(i, j, k)] += t[k]
 
 
-def last_kernel(coef, w_in, acc, ya, yb, xb, xa, v, out, obuf, sem):
+def last_kernel(coef, w_in, acc, ya, xb, yb, xa, v, out, obuf, sem):
     del w_in
     take_messages(v, xa, xb, ya, yb)
     started = []
@@ -586,7 +586,7 @@
         coef = coef * time_step / stage
         xa, xb = swap(xa, "gx", 0), swap(xb, "gx", 1)
         ya, yb = swap(ya, "gy", 0), swap(yb, "gy", 1)
-        got = [ya, yb, xb, xa]
+        got = [ya, xb, yb, xa]
         if stage == 1:
             acc, w, c2 = call(
                 functools.partial(local_first_kernel, coef),

time: 70 us -> 75.2 us (1.074); the launches traced: 68.7 us -> 75 us
  waiting for transfers between devices: 9.01 us -> 19.9 us
  starting transfers between devices: 20.1 us -> 15.6 us
    ppermute x16, waiting for transfers between devices: 9.01 us -> 19.9 us  [swap(): return lax.ppermute(x, axis, pairs(lax.axis_size(axis), offset))]
    ppermute x16, starting transfers between devices: 20.1 us -> 15.6 us  [swap(): return lax.ppermute(x, axis, pairs(lax.axis_size(axis), offset))]
  transfers between devices with their start and end apart: 16 -> 16, of which waited for: 6 -> 9; matrix products, arithmetic and copies ran while one was open for 0% -> 0% of each run, Pallas kernels for 10% -> 10%
where the time goes in v3:
time: 75.2 us; the launch traced here: 75 us
  blocking collectives  25.2 us (34%)
  waiting for transfers between devices  19.9 us (26%)
  starting transfers between devices  15.6 us (21%)
  Pallas kernels  13.4 us (18%)
    all_to_all x1, blocking collectives, body(): lax.all_to_all(table.reshape(devices, 1, 128), ('gx', 'gy'), 0, 0)  25.2 us
    ppermute x16, waiting for transfers between devices, swap(): return lax.ppermute(x, axis, pairs(lax.axis_size(axis), offset))  19.9 us
    ppermute x16, starting transfers between devices, swap(): return lax.ppermute(x, axis, pairs(lax.axis_size(axis), offset))  15.6 us
    pallas_call x10, Pallas kernels, call(): pl.pallas_call(kernel, out_shape=[jax.ShapeDtypeStruct(s, f32) for s in o...  13.4 us
  transfers between devices with their start and end apart: 16, of which 9 were waited for; matrix products, arithmetic and copies ran while one was open for 0% of the time, Pallas kernels for 10%

profile of v3, /device:TPU:1, one launch (start us, length us, event | category | flops | bytes accessed | tf_op | source)
XLA Modules:
  0.0 75.0 jit_solution(10131482752477078131)
XLA Ops:
  0.0 2.2 %shard_map.64 = (f32[125,8,256]{2,1,0:T(8,128)S(1)}, f32[125,8,256]{2,1,0:T(8,128)S(1)}, f32[250,256]{1,0:T(8,128)S(1)}, f32[250,256]{1,0:T(8,128)S(1)}) custom-call(f32[6,125,1,256]{3,2,1,0:T(1,128)} %bitcast.17, f32[6,125,1,256]{3,2,1,0:T(1,128)} %bitcast.18), custom_call_target="tpu_custom_call" | custom-call | bytes 4096000 | tf_op jit(solution)/shard_map/pallas_call | solution.py:519
  2.2 3.3 %collective-permute-start = (f32[250,256]{1,0:T(8,128)S(1)}, f32[250,256]{1,0:T(8,128)S(1)}, u32[]{:S(2)}, u32[]{:S(2)}) collective-permute-start(f32[250,256]{1,0:T(8,128)S(1)} %get-tuple-element.51), channel_id=1, source_target_pairs={{0,16},{16,0},{32,48},{48,32},{64,80},{80,64},{96,112},{112,96},{1... | collective-permute-start | bytes 768008 | tf_op jit(solution)/shard_map/ppermute | solution.py:540
  5.6 0.0 collective-permute-start.1
  5.6 0.0 copy-start
  5.6 0.0 copy-start.1
  5.6 0.0 copy-start.2
  5.6 0.0 copy-start.3
  5.6 0.7 copy-done
  6.2 0.0 copy-done.1
  6.2 0.0 copy-done.2
  6.2 0.0 copy-done.3
  6.3 3.0 %shard_map.65 = (f32[256,128]{1,0:T(8,128)S(1)}, f32[125,6,256]{2,1,0:T(8,128)S(1)}, f32[125,6,256]{2,1,0:T(8,128)S(1)}, f32[125,6,256]{2,1,0:T(8,128)S(1)}, f32[125,6,256]{2,1,0:T(8,128)S(1)}) custom-call(f32[125,8,256]{2,1,0:T(8,128)S(1)} %get-tuple-element.45.u8, f32[125,8,256]{2,1,0:T(8,128)S(1)} %get-tuple-element.46.cbuf, s32[1,100]{1,0:T(1,128)S(1)} %bitcast.14, ...), custom_call_target="tpu_custom_call" | custom-call | bytes 5253472 | tf_op jit(solution)/shard_map/pallas_call | solution.py:519
  9.3 0.0 collective-permute-done.xa
  9.3 2.4 %collective-permute-done.1.xb = f32[250,256]{1,0:T(8,128)S(1)} collective-permute-done((f32[250,256]{1,0:T(8,128)S(1)}, f32[250,256]{1,0:T(8,128)S(1)}, u32[]{:S(2)}, u32[]{:S(2)}) %collective-permute-start.1) | collective-permute-done | bytes 256032 | tf_op jit(solution)/shard_map/ppermute | solution.py:540
  11.6 0.2 shard_map.66
  11.9 0.1 collective-permute-start.2
  12.0 3.3 %collective-permute-start.3 = (f32[270,256]{1,0:T(8,128)S(1)}, f32[270,256]{1,0:T(8,128)S(1)}, u32[]{:S(2)}, u32[]{:S(2)}) collective-permute-start(f32[270,256]{1,0:T(8,128)S(1)} %get-tuple-element.57), channel_id=1, source_target_pairs={{1,2},{2,1},{3,4},{4,3},{5,6},{6,5},{7,8},{8,7},{9,10},{10,9},{11,... | collective-permute-start | bytes 829448 | tf_op jit(solution)/shard_map/ppermute | solution.py:540
  15.3 25.2 %all_to_all.5 = f32[256,1,128]{2,1,0:T(1,128)S(1)} all-to-all(f32[256,1,128]{2,1,0:T(1,128)S(1)} %bitcast.13), channel_id=1, replica_groups=mesh['gx'=16,'gy'=16] {'gx','gy'}, dimensions={0} | all-to-all | bytes 262144 | tf_op jit(solution)/shard_map/all_to_all | solution.py:576
  40.5 0.0 collective-permute-done.2.ya
  40.5 0.0 collective-permute-done.3.yb
  40.5 1.6 %shard_map.67 = (f32[125,6,256]{2,1,0:T(8,128)S(1)}, f32[125,6,256]{2,1,0:T(8,128)S(1)}, f32[125,6,256]{2,1,0:T(8,128)S(1)}, f32[49,6,256]{2,1,0:T(8,128)S(1)}, ...) custom-call(f32[125,6,256]{2,1,0:T(8,128)S(1)} %get-tuple-element.47, ...), custom_call_target="tpu_custom_call", output_to_operand_aliasing={{0}: (0, {}), {1}: (1, {}), {2}: (2, {})} | custom-call | bytes 7487488 | tf_op jit(solution)/shard_map/pallas_call | solution.py:519
  42.1 0.4 collective-permute-start.4
  42.5 1.2 %collective-permute-start.5 = (f32[150,256]{1,0:T(8,128)S(1)}, f32[150,256]{1,0:T(8,128)S(1)}, u32[]{:S(2)}, u32[]{:S(2)}) collective-permute-start(f32[150,256]{1,0:T(8,128)S(1)} %get-tuple-element.65), channel_id=1, source_target_pairs={{16,32},{32,16},{48,64},{64,48},{80,96},{96,80},{112,128},{128,112... | collective-permute-start | bytes 460808 | tf_op jit(solution)/shard_map/ppermute | solution.py:540
  43.8 1.5 %collective-permute-start.6 = (f32[150,256]{1,0:T(8,128)S(1)}, f32[150,256]{1,0:T(8,128)S(1)}, u32[]{:S(2)}, u32[]{:S(2)}) collective-permute-start(f32[150,256]{1,0:T(8,128)S(1)} %get-tuple-element.66), channel_id=1, source_target_pairs={{1,2},{2,1},{3,4},{4,3},{5,6},{6,5},{7,8},{8,7},{9,10},{10,9},{11,... | collective-permute-start | bytes 460808 | tf_op jit(solution)/shard_map/ppermute | solution.py:540
  45.3 0.0 collective-permute-start.7
  45.3 1.6 %shard_map.68 = (f32[125,6,256]{2,1,0:T(8,128)S(1)}, f32[125,6,256]{2,1,0:T(8,128)S(1)}, f32[125,6,256]{2,1,0:T(8,128)S(1)}) custom-call(f32[125,6,256]{2,1,0:T(8,128)S(1)} %get-tuple-element.59.v, f32[125,6,256]{2,1,0:T(8,128)S(1)} %get-tuple-element.60.c0, f32[125,6,256]{2,1,0:T(8,128)S(1)} %get-tuple-element.61.c1, ...), custom_call_target="tpu_custom_call", output_to_operand_aliasing={{2}: (3, {})} | custom-call | flops 10000000 | bytes 7766016 | tf_op jit(solution)/shard_map/pallas_call | solution.py:519
  46.9 0.4 collective-permute-done.4.ya
  47.3 0.2 collective-permute-done.5.xb
  47.5 5.6 %collective-permute-done.6.yb = f32[150,256]{1,0:T(8,128)S(1)} collective-permute-done((f32[150,256]{1,0:T(8,128)S(1)}, f32[150,256]{1,0:T(8,128)S(1)}, u32[]{:S(2)}, u32[]{:S(2)}) %collective-permute-start.6) | collective-permute-done | bytes 153632 | tf_op jit(solution)/shard_map/ppermute | solution.py:540
  53.1 0.0 collective-permute-done.7.xa
  53.1 0.5 shard_map.69
  53.6 0.1 collective-permute-start.8
  53.7 0.7 collective-permute-start.9
  54.4 1.3 %collective-permute-start.10 = (f32[150,256]{1,0:T(8,128)S(1)}, f32[150,256]{1,0:T(8,128)S(1)}, u32[]{:S(2)}, u32[]{:S(2)}) collective-permute-start(f32[150,256]{1,0:T(8,128)S(1)} %get-tuple-element.74), channel_id=1, source_target_pairs={{1,2},{2,1},{3,4},{4,3},{5,6},{6,5},{7,8},{8,7},{9,10},{10,9},{11,... | collective-permute-start | bytes 460808 | tf_op jit(solution)/shard_map/ppermute | solution.py:540
  55.7 0.4 collective-permute-start.11
  56.1 1.3 %shard_map.70 = (f32[125,6,256]{2,1,0:T(8,128)S(1)}, f32[125,6,256]{2,1,0:T(8,128)S(1)}) custom-call(f32[125,6,256]{2,1,0:T(8,128)S(1)} %get-tuple-element.68.v, f32[125,6,256]{2,1,0:T(8,128)S(1)} %get-tuple-element.60.c0, f32[125,6,256]{2,1,0:T(8,128)S(1)} %get-tuple-element.61.c1, ...), custom_call_target="tpu_custom_call", output_to_operand_aliasing={{0}: (4, {})} | custom-call | flops 10000000 | bytes 5376000 | tf_op jit(solution)/shard_map/pallas_call | solution.py:519
  57.4 1.4 %collective-permute-done.8.ya = f32[150,256]{1,0:T(8,128)S(1)} collective-permute-done((f32[150,256]{1,0:T(8,128)S(1)}, f32[150,256]{1,0:T(8,128)S(1)}, u32[]{:S(2)}, u32[]{:S(2)}) %collective-permute-start.8) | collective-permute-done | bytes 153632 | tf_op jit(solution)/shard_map/ppermute | solution.py:540
  58.8 0.0 collective-permute-done.9.xb
  58.8 4.6 %collective-permute-done.10.yb = f32[150,256]{1,0:T(8,128)S(1)} collective-permute-done((f32[150,256]{1,0:T(8,128)S(1)}, f32[150,256]{1,0:T(8,128)S(1)}, u32[]{:S(2)}, u32[]{:S(2)}) %collective-permute-start.10) | collective-permute-done | bytes 153632 | tf_op jit(solution)/shard_map/ppermute | solution.py:540
  63.4 0.0 collective-permute-done.11.xa
  63.4 0.4 shard_map.71
  63.8 0.1 collective-permute-start.12
  63.9 1.0 %collective-permute-start.13 = (f32[150,256]{1,0:T(8,128)S(1)}, f32[150,256]{1,0:T(8,128)S(1)}, u32[]{:S(2)}, u32[]{:S(2)}) collective-permute-start(f32[150,256]{1,0:T(8,128)S(1)} %get-tuple-element.81), channel_id=1, source_target_pairs={{16,32},{32,16},{48,64},{64,48},{80,96},{96,80},{112,128},{128,112... | collective-permute-start | bytes 460808 | tf_op jit(solution)/shard_map/ppermute | solution.py:540
  64.9 1.5 %collective-permute-start.14 = (f32[150,256]{1,0:T(8,128)S(1)}, f32[150,256]{1,0:T(8,128)S(1)}, u32[]{:S(2)}, u32[]{:S(2)}) collective-permute-start(f32[150,256]{1,0:T(8,128)S(1)} %get-tuple-element.82), channel_id=1, source_target_pairs={{1,2},{2,1},{3,4},{4,3},{5,6},{6,5},{7,8},{8,7},{9,10},{10,9},{11,... | collective-permute-start | bytes 460808 | tf_op jit(solution)/shard_map/ppermute | solution.py:540
  66.4 0.5 collective-permute-start.15
  66.9 1.3 %shard_map.72 = (f32[125,6,256]{2,1,0:T(8,128)S(1)}, f32[125,6,256]{2,1,0:T(8,128)S(1)}) custom-call(f32[125,6,256]{2,1,0:T(8,128)S(1)} %get-tuple-element.76.v, f32[125,6,256]{2,1,0:T(8,128)S(1)} %get-tuple-element.60.c0, f32[125,6,256]{2,1,0:T(8,128)S(1)} %get-tuple-element.61.c1, ...), custom_call_target="tpu_custom_call", output_to_operand_aliasing={{0}: (4, {})} | custom-call | flops 10000000 | bytes 5376000 | tf_op jit(solution)/shard_map/pallas_call | solution.py:519
  68.2 0.5 collective-permute-done.12.ya
  68.7 0.3 collective-permute-done.13.xb
  69.0 4.6 %collective-permute-done.14.yb = f32[150,256]{1,0:T(8,128)S(1)} collective-permute-done((f32[150,256]{1,0:T(8,128)S(1)}, f32[150,256]{1,0:T(8,128)S(1)}, u32[]{:S(2)}, u32[]{:S(2)}) %collective-permute-start.14) | collective-permute-done | bytes 153632 | tf_op jit(solution)/shard_map/ppermute | solution.py:540
  73.6 0.0 collective-permute-done.15.xa
  73.6 1.3 %shard_map.73 = (f32[125,6,256]{2,1,0:T(8,128)S(1)}, f32[6,125,1,256]{3,2,1,0:T(1,128)}) custom-call(f32[125,6,256]{2,1,0:T(8,128)S(1)} %get-tuple-element.78.w_in, f32[125,6,256]{2,1,0:T(8,128)S(1)} %get-tuple-element.79.acc, f32[150,256]{1,0:T(8,128)S(1)} %collective-permute-done.12.ya, ...), custom_call_target="tpu_custom_call", output_to_operand_aliasing={{0}: (0, {})} | custom-call | bytes 3686400 | tf_op jit(solution)/shard_map/pallas_call | solution.py:519
Async XLA Ops:
  2.2 7.1 %collective-permute-start = (f32[250,256]{1,0:T(8,128)S(1)}, f32[250,256]{1,0:T(8,128)S(1)}, u32[]{:S(2)}, u32[]{:S(2)}) collective-permute-start(f32[250,256]{1,0:T(8,128)S(1)} %get-tuple-element.51), channel_id=1, source_target_pairs={{0,16},{16,0},{32,48},{48,32},{64,80},{80,64},{96,112},{112,96},{1... | collective-permute-start | bytes 768008 | tf_op jit(solution)/shard_map/ppermute | solution.py:540
  5.6 6.1 %collective-permute-start.1 = (f32[250,256]{1,0:T(8,128)S(1)}, f32[250,256]{1,0:T(8,128)S(1)}, u32[]{:S(2)}, u32[]{:S(2)}) collective-permute-start(f32[250,256]{1,0:T(8,128)S(1)} %get-tuple-element.52), channel_id=1, source_target_pairs={{16,32},{32,16},{48,64},{64,48},{80,96},{96,80},{112,128},{128,112... | collective-permute-start | bytes 768008 | tf_op jit(solution)/shard_map/ppermute | solution.py:540
  5.6 0.7 copy-start
  5.6 0.7 copy-start.1
  5.6 0.7 copy-start.2
  5.6 0.7 copy-start.3
  11.9 28.7 %collective-permute-start.2 = (f32[270,256]{1,0:T(8,128)S(1)}, f32[270,256]{1,0:T(8,128)S(1)}, u32[]{:S(2)}, u32[]{:S(2)}) collective-permute-start(f32[270,256]{1,0:T(8,128)S(1)} %get-tuple-element.56), channel_id=1, source_target_pairs={{0,1},{1,0},{2,3},{3,2},{4,5},{5,4},{6,7},{7,6},{8,9},{9,8},{10,11... | collective-permute-start | bytes 829448 | tf_op jit(solution)/shard_map/ppermute | solution.py:540
  12.0 28.6 %collective-permute-start.3 = (f32[270,256]{1,0:T(8,128)S(1)}, f32[270,256]{1,0:T(8,128)S(1)}, u32[]{:S(2)}, u32[]{:S(2)}) collective-permute-start(f32[270,256]{1,0:T(8,128)S(1)} %get-tuple-element.57), channel_id=1, source_target_pairs={{1,2},{2,1},{3,4},{4,3},{5,6},{6,5},{7,8},{8,7},{9,10},{10,9},{11,... | collective-permute-start | bytes 829448 | tf_op jit(solution)/shard_map/ppermute | solution.py:540
  42.1 5.2 %collective-permute-start.4 = (f32[150,256]{1,0:T(8,128)S(1)}, f32[150,256]{1,0:T(8,128)S(1)}, u32[]{:S(2)}, u32[]{:S(2)}) collective-permute-start(f32[150,256]{1,0:T(8,128)S(1)} %get-tuple-element.64), channel_id=1, source_target_pairs={{0,1},{1,0},{2,3},{3,2},{4,5},{5,4},{6,7},{7,6},{8,9},{9,8},{10,11... | collective-permute-start | bytes 460808 | tf_op jit(solution)/shard_map/ppermute | solution.py:540
  42.5 5.0 %collective-permute-start.5 = (f32[150,256]{1,0:T(8,128)S(1)}, f32[150,256]{1,0:T(8,128)S(1)}, u32[]{:S(2)}, u32[]{:S(2)}) collective-permute-start(f32[150,256]{1,0:T(8,128)S(1)} %get-tuple-element.65), channel_id=1, source_target_pairs={{16,32},{32,16},{48,64},{64,48},{80,96},{96,80},{112,128},{128,112... | collective-permute-start | bytes 460808 | tf_op jit(solution)/shard_map/ppermute | solution.py:540
  43.8 9.3 %collective-permute-start.6 = (f32[150,256]{1,0:T(8,128)S(1)}, f32[150,256]{1,0:T(8,128)S(1)}, u32[]{:S(2)}, u32[]{:S(2)}) collective-permute-start(f32[150,256]{1,0:T(8,128)S(1)} %get-tuple-element.66), channel_id=1, source_target_pairs={{1,2},{2,1},{3,4},{4,3},{5,6},{6,5},{7,8},{8,7},{9,10},{10,9},{11,... | collective-permute-start | bytes 460808 | tf_op jit(solution)/shard_map/ppermute | solution.py:540
  45.3 7.8 %collective-permute-start.7 = (f32[150,256]{1,0:T(8,128)S(1)}, f32[150,256]{1,0:T(8,128)S(1)}, u32[]{:S(2)}, u32[]{:S(2)}) collective-permute-start(f32[150,256]{1,0:T(8,128)S(1)} %get-tuple-element.67), channel_id=1, source_target_pairs={{0,16},{16,0},{32,48},{48,32},{64,80},{80,64},{96,112},{112,96},{1... | collective-permute-start | bytes 460808 | tf_op jit(solution)/shard_map/ppermute | solution.py:540
  53.6 5.2 %collective-permute-start.8 = (f32[150,256]{1,0:T(8,128)S(1)}, f32[150,256]{1,0:T(8,128)S(1)}, u32[]{:S(2)}, u32[]{:S(2)}) collective-permute-start(f32[150,256]{1,0:T(8,128)S(1)} %get-tuple-element.72), channel_id=1, source_target_pairs={{0,1},{1,0},{2,3},{3,2},{4,5},{5,4},{6,7},{7,6},{8,9},{9,8},{10,11... | collective-permute-start | bytes 460808 | tf_op jit(solution)/shard_map/ppermute | solution.py:540
  53.7 5.2 %collective-permute-start.9 = (f32[150,256]{1,0:T(8,128)S(1)}, f32[150,256]{1,0:T(8,128)S(1)}, u32[]{:S(2)}, u32[]{:S(2)}) collective-permute-start(f32[150,256]{1,0:T(8,128)S(1)} %get-tuple-element.73), channel_id=1, source_target_pairs={{16,32},{32,16},{48,64},{64,48},{80,96},{96,80},{112,128},{128,112... | collective-permute-start | bytes 460808 | tf_op jit(solution)/shard_map/ppermute | solution.py:540
  54.4 9.0 %collective-permute-start.10 = (f32[150,256]{1,0:T(8,128)S(1)}, f32[150,256]{1,0:T(8,128)S(1)}, u32[]{:S(2)}, u32[]{:S(2)}) collective-permute-start(f32[150,256]{1,0:T(8,128)S(1)} %get-tuple-element.74), channel_id=1, source_target_pairs={{1,2},{2,1},{3,4},{4,3},{5,6},{6,5},{7,8},{8,7},{9,10},{10,9},{11,... | collective-permute-start | bytes 460808 | tf_op jit(solution)/shard_map/ppermute | solution.py:540
  55.7 7.7 %collective-permute-start.11 = (f32[150,256]{1,0:T(8,128)S(1)}, f32[150,256]{1,0:T(8,128)S(1)}, u32[]{:S(2)}, u32[]{:S(2)}) collective-permute-start(f32[150,256]{1,0:T(8,128)S(1)} %get-tuple-element.75), channel_id=1, source_target_pairs={{0,16},{16,0},{32,48},{48,32},{64,80},{80,64},{96,112},{112,96},{1... | collective-permute-start | bytes 460808 | tf_op jit(solution)/shard_map/ppermute | solution.py:540
  63.8 4.9 %collective-permute-start.12 = (f32[150,256]{1,0:T(8,128)S(1)}, f32[150,256]{1,0:T(8,128)S(1)}, u32[]{:S(2)}, u32[]{:S(2)}) collective-permute-start(f32[150,256]{1,0:T(8,128)S(1)} %get-tuple-element.80), channel_id=1, source_target_pairs={{0,1},{1,0},{2,3},{3,2},{4,5},{5,4},{6,7},{7,6},{8,9},{9,8},{10,11... | collective-permute-start | bytes 460808 | tf_op jit(solution)/shard_map/ppermute | solution.py:540
  63.9 5.0 %collective-permute-start.13 = (f32[150,256]{1,0:T(8,128)S(1)}, f32[150,256]{1,0:T(8,128)S(1)}, u32[]{:S(2)}, u32[]{:S(2)}) collective-permute-start(f32[150,256]{1,0:T(8,128)S(1)} %get-tuple-element.81), channel_id=1, source_target_pairs={{16,32},{32,16},{48,64},{64,48},{80,96},{96,80},{112,128},{128,112... | collective-permute-start | bytes 460808 | tf_op jit(solution)/shard_map/ppermute | solution.py:540
  64.9 8.7 %collective-permute-start.14 = (f32[150,256]{1,0:T(8,128)S(1)}, f32[150,256]{1,0:T(8,128)S(1)}, u32[]{:S(2)}, u32[]{:S(2)}) collective-permute-start(f32[150,256]{1,0:T(8,128)S(1)} %get-tuple-element.82), channel_id=1, source_target_pairs={{1,2},{2,1},{3,4},{4,3},{5,6},{6,5},{7,8},{8,7},{9,10},{10,9},{11,... | collective-permute-start | bytes 460808 | tf_op jit(solution)/shard_map/ppermute | solution.py:540
  66.4 7.1 %collective-permute-start.15 = (f32[150,256]{1,0:T(8,128)S(1)}, f32[150,256]{1,0:T(8,128)S(1)}, u32[]{:S(2)}, u32[]{:S(2)}) collective-permute-start(f32[150,256]{1,0:T(8,128)S(1)} %get-tuple-element.83), channel_id=1, source_target_pairs={{0,16},{16,0},{32,48},{48,32},{64,80},{80,64},{96,112},{112,96},{1... | collective-permute-start | bytes 460808 | tf_op jit(solution)/shard_map/ppermute | solution.py:540
